TPU v7x, 128 devices: a whole 4x4x4 slice. The times are simulated.
128 devices in a mesh: dom: 32 (over z, y, core), grp: 4 (over x).
Axes of the slice: x: 4, y: 4, z: 4, core: 2. Of those that a mesh axis runs over, the one named last changes fastest.
Arguments:
- a_blocks: bfloat16 [128, 7, 48, 64, 448], P('dom', None, 'grp'), may hold values from -0.25 to 0.25
- prolong: bfloat16 [128, 7, 48, 64, 128], P('dom', None, 'grp'), may hold values from -0.75 to 0.75
- zagg: int32 [128], replicated, may hold values from 0 to 63, as said below
- xlen: int32 [4, 4], replicated, may hold values from 1 to 6, 12 in all within a row
Outputs:
- coarse_operator: bfloat16 [64, 16, 128, 640], P('dom', 'grp')
Inputs may be any that keep to these rules, and one draw needn't show every extreme that they name: zagg starts at 0, never falls and rises by 0 or 1 from layer to layer; every run of 4 layers of one index of dom holds exactly 2 layers where a new interval begins, the first layer of all among them.
All inputs are finite; a program needn't handle non-finite values.
Results may differ from a plain program's by a relative error of at most 0.005.
Values may be sent and summed in bfloat16 or wider, within the bound.
A program may use at most 256 MiB of HBM per device.

v0:
```python
import jax
import jax.numpy as jnp
from jax import lax
from jax.sharding import PartitionSpec as P


def with_halo(block, sides, width):
    for axis, dim in sides:
        count = lax.axis_size(axis)
        forward = [(i, i + 1) for i in range(count - 1)]
        backward = [(target, source) for source, target in forward]
        low = lax.ppermute(
            lax.slice_in_dim(block, block.shape[dim] - width, None, axis=dim), axis, forward
        )
        high = lax.ppermute(lax.slice_in_dim(block, 0, width, axis=dim), axis, backward)
        block = jnp.concatenate([low, block, high], axis=dim)
    return block


def passed_along(block, axis, distance):
    devices = range(lax.axis_size(axis))
    route = [(i - distance, i) for i in devices if i - distance in devices]
    return lax.ppermute(block, axis, route)


def neighbour_products(a_blocks, padded):
    width = a_blocks.shape[-1] // 7
    centre = padded[1:-1, 1:-1, 1:-1]
    beside = [
        centre,
        padded[1:-1, 1:-1, :-2],
        padded[1:-1, 1:-1, 2:],
        padded[1:-1, :-2, 1:-1],
        padded[1:-1, 2:, 1:-1],
        padded[:-2, 1:-1, 1:-1],
        padded[2:, 1:-1, 1:-1],
    ]
    return [
        jnp.einsum(
            "zyxrs,zyxsc->zyxrc",
            a_blocks[..., k * width : (k + 1) * width],
            beside[k],
            preferred_element_type=jnp.float32,
        )
        for k in range(7)
    ]


def route_slots(products, same_xm, same_xp, same_zm, same_zp):
    self_sum = (
        products[0]
        + products[3]
        + products[4]
        + same_xm * products[1]
        + same_xp * products[2]
        + same_zm * products[5]
        + same_zp * products[6]
    )
    slots = [
        self_sum,
        (1.0 - same_xm) * products[1],
        (1.0 - same_xp) * products[2],
        (1.0 - same_zm) * products[5],
        (1.0 - same_zp) * products[6],
    ]
    return jnp.concatenate(slots, axis=-1).astype(jnp.bfloat16)


def per_device(a_blocks, prolong, zagg, xlen):
    layers, depth, columns, block, coarse_width = prolong.shape
    intervals = xlen.shape[1]
    halves = layers // 2
    layer_dev = lax.axis_index("dom")
    column_dev = lax.axis_index("grp")
    row_lengths = lax.dynamic_index_in_dim(xlen, column_dev, 0, keepdims=False)
    ends = jnp.cumsum(row_lengths)
    within = jnp.sum(
        (ends[:, None] <= jnp.arange(columns, dtype=jnp.int32)[None, :]).astype(jnp.int32), axis=0
    )
    column_pad = jnp.pad(within, 1, constant_values=-1)
    same_xm = (column_pad[:-2] == within).astype(jnp.float32).reshape(1, 1, columns, 1, 1)
    same_xp = (column_pad[2:] == within).astype(jnp.float32).reshape(1, 1, columns, 1, 1)
    layer_pad = jnp.pad(zagg, 1, constant_values=-1)
    layer_ids = lax.dynamic_slice_in_dim(layer_pad, layer_dev * layers, layers + 2, 0)
    same_zm = (layer_ids[:-2] == layer_ids[1:-1]).astype(jnp.float32).reshape(layers, 1, 1, 1, 1)
    same_zp = (layer_ids[2:] == layer_ids[1:-1]).astype(jnp.float32).reshape(layers, 1, 1, 1, 1)
    rimmed = with_halo(prolong, (("dom", 0), ("grp", 2)), 1)
    padded = jnp.pad(rimmed, ((0, 0), (1, 1), (0, 0), (0, 0), (0, 0)))
    products = neighbour_products(a_blocks, padded)
    routed = route_slots(products, same_xm, same_xp, same_zm, same_zp)
    member = (within[None, :] == jnp.arange(intervals, dtype=jnp.int32)[:, None]).astype(
        jnp.bfloat16
    )
    local_ids = layer_ids[1:-1] - layer_dev * halves + 1

    def accumulate(layer, running):
        piece = lax.dynamic_index_in_dim(prolong, layer, 0, keepdims=False)
        slots = lax.dynamic_index_in_dim(routed, layer, 0, keepdims=False)
        masked = piece[None] * member[:, None, :, None, None]
        coarse = jnp.einsum("eyxrc,yxrk->eck", masked, slots, preferred_element_type=jnp.float32)
        target = local_ids[layer]
        current = lax.dynamic_index_in_dim(running, target, 0, keepdims=True)
        return lax.dynamic_update_index_in_dim(running, current + coarse[None], target, 0)

    start = jnp.zeros((halves + 1, intervals, coarse_width, 5 * coarse_width), jnp.float32)
    running = lax.fori_loop(0, layers, accumulate, start)
    carried = passed_along(running[0], "dom", -1)
    owned = running[1:]
    finished = jnp.concatenate([owned[:-1], owned[-1:] + carried[None]], axis=0)
    return finished.astype(jnp.bfloat16)


def solution(mesh):
    in_specs = (P("dom", None, "grp", None, None), P("dom", None, "grp", None, None), P(), P())
    out_specs = P("dom", "grp", None, None)
    return jax.shard_map(
        per_device, mesh=mesh, in_specs=in_specs, out_specs=out_specs, check_vma=False
    )
```

profile of v0, /device:TPU:27, one launch (start us, length us, event | category | flops | bytes accessed | tf_op | source)
XLA Modules:
  0.0 225.4 jit_solution(4747937951273942634)
XLA Ops:
  0.0 0.0 copy-start
  0.0 0.0 slice-start
  0.0 4.1 %fusion.66 = (bf16[1,7,12,64,128]{4,3,2,1,0:T(8,128)(2,1)}, bf16[1,7,12,64,128]{4,3,2,1,0:T(8,128)(2,1)}) fusion(bf16[4,7,12,64,128]{4,3,2,1,0:T(8,128)(2,1)} %param.7), kind=kLoop, calls=%fused_computation.93 | loop fusion | bytes 5505024 | tf_op jit(solution)/shard_map/slice | solution.py:13
  4.1 3.8 %collective-permute-start = (bf16[1,7,12,64,128]{4,3,2,1,0:T(8,128)(2,1)}, bf16[1,7,12,64,128]{4,3,2,1,0:T(8,128)(2,1)S(1)}, u32[]{:S(2)}, u32[]{:S(2)}) collective-permute-start(bf16[1,7,12,64,128]{4,3,2,1,0:T(8,128)(2,1)} %get-tuple-element.164), channel_id=1, source_target_pairs={{0,4},{4,8},{8,12},{12,16},{16,20},{20,24},{24,28},{28,32},{32,36}... | collective-permute-start | bytes 4128776 | tf_op jit(solution)/shard_map/ppermute | solution.py:12
  7.9 1.9 collective-permute-start.1
  9.8 0.7 pad_dynamic-slice_fusion
  10.6 0.1 broadcast_subtract_fusion.1
  10.6 0.0 copy-done
  10.6 0.2 reduce-window.8
  10.8 0.1 convert_reduce_fusion
  10.9 0.1 broadcast_subtract_fusion.3
  11.0 0.1 subtract_add_fusion
  11.1 0.0 slice-start.1
  11.1 10.0 %fusion.58 = f32[4,7,12,64,128]{4,3,2,1,0:T(8,128)} fusion(bf16[4,7,12,64,128]{4,3,2,1,0:T(8,128)(2,1)} %param.7, bf16[4,7,12,64,448]{4,3,2,1,0:T(8,128)(2,1)} %param.6), kind=kOutput, calls=%fused_computation.65 | convolution fusion | flops 352321536 | bytes 22020096 | tf_op jit(solution)/shard_map/zyxrs,zyxsc->zyxrc/dot_general | solution.py:39
  21.1 2.3 %collective-permute-done = bf16[1,7,12,64,128]{4,3,2,1,0:T(8,128)(2,1)S(1)} collective-permute-done((bf16[1,7,12,64,128]{4,3,2,1,0:T(8,128)(2,1)}, bf16[1,7,12,64,128]{4,3,2,1,0:T(8,128)(2,1)S(1)}, u32[]{:S(2)}, u32[]{:S(2)}) %collective-permute-start) | collective-permute-done | bytes 1376288 | tf_op jit(solution)/shard_map/ppermute | solution.py:12
  23.4 0.1 constant_dynamic-update-slice_fusion.2
  23.6 0.0 slice-done
  23.6 0.0 slice-done.1
  23.6 2.1 constant_dynamic-update-slice_fusion.1
  25.7 4.3 %collective-permute-done.1 = bf16[1,7,12,64,128]{4,3,2,1,0:T(8,128)(2,1)} collective-permute-done((bf16[1,7,12,64,128]{4,3,2,1,0:T(8,128)(2,1)}, bf16[1,7,12,64,128]{4,3,2,1,0:T(8,128)(2,1)}, u32[]{:S(2)}, u32[]{:S(2)}) %collective-permute-start.1) | collective-permute-done | bytes 1376288 | tf_op jit(solution)/shard_map/ppermute | solution.py:15
  29.9 1.6 constant_dynamic-update-slice_fusion
  31.5 1.2 fusion.65
  32.7 3.1 %collective-permute-start.2 = (bf16[6,7,1,64,128]{4,3,2,1,0:T(8,128)(2,1)}, bf16[6,7,1,64,128]{4,3,2,1,0:T(8,128)(2,1)S(1)}, u32[]{:S(2)}, u32[]{:S(2)}) collective-permute-start(bf16[6,7,1,64,128]{4,3,2,1,0:T(8,128)(2,1)} %get-tuple-element.162), channel_id=1, source_target_pairs={{0,1},{1,2},{2,3},{4,5},{5,6},{6,7},{8,9},{9,10},{10,11},{12,13},{... | collective-permute-start | bytes 2064392 | tf_op jit(solution)/shard_map/ppermute | solution.py:12
  35.8 2.4 %collective-permute-start.3 = (bf16[6,7,1,64,128]{4,3,2,1,0:T(8,128)(2,1)}, bf16[6,7,1,64,128]{4,3,2,1,0:T(8,128)(2,1)}, u32[]{:S(2)}, u32[]{:S(2)}) collective-permute-start(bf16[6,7,1,64,128]{4,3,2,1,0:T(8,128)(2,1)} %get-tuple-element.163), channel_id=1, source_target_pairs={{1,0},{2,1},{3,2},{5,4},{6,5},{7,6},{9,8},{10,9},{11,10},{13,12},{... | collective-permute-start | bytes 2064392 | tf_op jit(solution)/shard_map/ppermute | solution.py:15
  38.2 8.7 %fusion.40 = f32[4,7,12,128,64]{3,4,2,1,0:T(8,128)} fusion(bf16[1,7,12,64,128]{4,3,2,1,0:T(8,128)(2,1)} %collective-permute-done.1, bf16[4,7,12,64,128]{4,3,2,1,0:T(8,128)(2,1)S(1)} %bitcast.100, bf16[4,7,12,64,448]{4,3,2,1,0:T(8,128)(2,1)} %param.6), kind=kOutput, calls=%fused_computation.44 | convolution fusion | flops 363331584 | bytes 23396352 | tf_op jit(solution)/shard_map/zyxrs,zyxsc->zyxrc/dot_general | solution.py:39
  46.9 8.4 %fusion.42 = f32[4,7,12,128,64]{3,4,2,1,0:T(8,128)} fusion(bf16[4,7,12,64,128]{4,3,2,1,0:T(8,128)(2,1)S(1)} %bitcast.100, bf16[1,7,12,64,128]{4,3,2,1,0:T(8,128)(2,1)S(1)} %collective-permute-done, bf16[4,7,12,64,448]{4,3,2,1,0:T(8,128)(2,1)} %param.6), kind=kOutput, calls=%fused_computation.47 | convolution fusion | flops 363331584 | bytes 23396352 | tf_op jit(solution)/shard_map/zyxrs,zyxsc->zyxrc/dot_general | solution.py:39
  55.3 0.0 collective-permute-done.2
  55.3 0.0 collective-permute-done.3
  55.3 6.8 %fusion.29 = bf16[6,9,14,64,128]{4,3,2,1,0:T(8,128)(2,1)} fusion(bf16[6,7,1,64,128]{4,3,2,1,0:T(8,128)(2,1)} %collective-permute-done.3, bf16[6,7,12,64,128]{4,3,2,1,0:T(8,128)(2,1)S(1)} %constant_dynamic-update-slice_fusion, bf16[6,7,1,64,128]{4,3,2,1,0:T(8,128)(2,1)S(1)} %collective-permute-done.2), kind=kLoop, calls=%fused_computation.22 | loop fusion | flops 74317824 | bytes 22020096 | tf_op jit(solution)/shard_map/concatenate | solution.py:16
  62.1 9.9 %fusion.50 = f32[4,7,12,128,64]{3,4,2,1,0:T(8,128)} fusion(bf16[6,9,14,64,128]{4,3,2,1,0:T(8,128)(2,1)} %fusion.29, bf16[4,7,12,64,448]{4,3,2,1,0:T(8,128)(2,1)} %param.6), kind=kOutput, calls=%fused_computation.57 | convolution fusion | flops 352321536 | bytes 22020096 | tf_op jit(solution)/shard_map/zyxrs,zyxsc->zyxrc/dot_general | solution.py:39
  72.0 8.5 %fusion.46 = f32[4,7,12,128,64]{3,4,2,1,0:T(8,128)} fusion(bf16[6,7,12,64,128]{4,3,2,1,0:T(8,128)(2,1)S(1)} %constant_dynamic-update-slice_fusion, bf16[6,7,1,64,128]{4,3,2,1,0:T(8,128)(2,1)S(1)} %collective-permute-done.2, bf16[4,7,12,64,448]{4,3,2,1,0:T(8,128)(2,1)} %param.6), kind=kOutput, calls=%fused_computation.53 | convolution fusion | flops 363331584 | bytes 25460736 | tf_op jit(solution)/shard_map/zyxrs,zyxsc->zyxrc/dot_general | solution.py:39
  80.5 8.3 %fusion.44 = f32[4,7,12,128,64]{3,4,2,1,0:T(8,128)} fusion(bf16[6,7,1,64,128]{4,3,2,1,0:T(8,128)(2,1)} %collective-permute-done.3, bf16[6,7,12,64,128]{4,3,2,1,0:T(8,128)(2,1)S(1)} %constant_dynamic-update-slice_fusion, bf16[4,7,12,64,448]{4,3,2,1,0:T(8,128)(2,1)} %param.6), kind=kOutput, calls=%fused_computation.50 | convolution fusion | flops 363331584 | bytes 25460736 | tf_op jit(solution)/shard_map/zyxrs,zyxsc->zyxrc/dot_general | solution.py:39
  88.9 27.5 %fusion.39 = bf16[4,7,12,64,640]{4,3,2,1,0:T(8,128)(2,1)} fusion(f32[4,7,12,128,64]{3,4,2,1,0:T(8,128)} %fusion.40, f32[4,7,12,128,64]{3,4,2,1,0:T(8,128)} %fusion.42, f32[4,7,12,128,64]{3,4,2,1,0:T(8,128)} %fusion.44, f32[4,7,12,128,64]{3,4,2,1,0:T(8,128)} %fusion.46, f32[4,7,12,64,128]{4,3,2,1,0:T(8,128)} %fusion.58, f32[4,7,12,128,64]{3,4,2,1,0:T(8,128)} %fusion.50, ...), kind=kOutput, calls=%fused_computation.42 | convolution fusion | flops 382599168 | bytes 82575488 | tf_op jit(solution)/shard_map/zyxrs,zyxsc->zyxrc/dot_general | solution.py:39
  116.4 8.4 %fusion.32 = bf16[4,7,12,64,640]{4,3,2,1,0:T(8,128)(2,1)} fusion(bf16[4,7,12,64,640]{4,3,2,1,0:T(8,128)(2,1)} %fusion.39, f32[4,7,12,128,64]{3,4,2,1,0:T(8,128)} %fusion.46, f32[12]{0:T(128)S(1)} %get-tuple-element.160), kind=kLoop, calls=%fused_computation.35 | loop fusion | flops 5505024 | bytes 16515120
  124.8 0.0 slice-start.2
  124.8 0.0 slice-start.3
  124.8 8.5 %fusion.34 = bf16[4,7,12,64,640]{4,3,2,1,0:T(8,128)(2,1)} fusion(bf16[4,7,12,64,640]{4,3,2,1,0:T(8,128)(2,1)} %fusion.32, f32[4,7,12,128,64]{3,4,2,1,0:T(8,128)} %fusion.44, f32[12]{0:T(128)S(1)} %get-tuple-element.166), kind=kLoop, calls=%fused_computation.37 | loop fusion | flops 5505024 | bytes 16515120
  133.3 0.0 slice-start.4
  133.3 8.5 %fusion.36 = bf16[4,7,12,64,640]{4,3,2,1,0:T(8,128)(2,1)} fusion(bf16[4,7,12,64,640]{4,3,2,1,0:T(8,128)(2,1)} %fusion.34, f32[4,7,12,128,64]{3,4,2,1,0:T(8,128)} %fusion.42, f32[4]{0:T(128)S(1)} %get-tuple-element.156), kind=kLoop, calls=%fused_computation.39 | loop fusion | flops 5505024 | bytes 16515088
  141.8 0.0 slice-done.2
  141.8 0.0 slice-done.3
  141.8 0.0 slice-done.4
  141.9 4.3 %fusion.38 = bf16[4,7,12,64,640]{4,3,2,1,0:T(8,128)(2,1)} fusion(bf16[4,7,12,64,640]{4,3,2,1,0:T(8,128)(2,1)} %fusion.36, f32[4,7,12,128,64]{3,4,2,1,0:T(8,128)S(1)} %bitcast.102, f32[4]{0:T(128)S(1)} %get-tuple-element.168), kind=kLoop, calls=%fused_computation.41 | loop fusion | flops 5505024 | bytes 16515088 | tf_op jit(solution)/shard_map/concatenate | solution.py:66
  146.2 2.4 %broadcast_in_dim.21 = f32[3,4,128,640]{3,2,1,0:T(8,128)} broadcast(f32[]{:T(128)} %constant.67.clone.1), dimensions={} | broadcast | bytes 3932164 | tf_op jit(solution)/shard_map/broadcast_in_dim | solution.py:105
  148.5 51.8 %while.14 = (s32[]{:T(128)}, f32[3,4,128,640]{3,2,1,0:T(8,128)}, s32[4]{0:T(128)S(1)}, bf16[4,7,12,64,128]{4,3,2,1,0:T(8,128)(2,1)}, bf16[4,7,12,64,640]{4,3,2,1...) while((s32[]{:T(128)}, f32[3,4,128,640]{3,2,1,0:T(8,128)}, ...), condition=%wide.region_3.4_spmd.clone, body=%wide.region_2.3_spmd.clone.sunk | while | flops 3526295552 | bytes 13632895 | solution.py:106
  148.5 0.6 dynamic_slice.59
  151.1 1.4 copy_bitcast_fusion.2
  152.5 8.9 %fusion.75 = f32[3,4,128,640]{3,2,1,0:T(8,128)} fusion(f32[3,4,128,640]{3,2,1,0:T(8,128)} %get-tuple-element.217, s32[]{:T(128)S(6)} %select_n.30, bf16[4,12]{1,0:T(4,128)(2,1)S(1)} %fusion.74, bf16[7,12,64,128]{3,2,0,1:T(8,128)(2,1)S(1)} %copy_bitcast_fusion.2, bf16[4,7,12,64,640]{4,3,2,1,0:T(8,128)(2,1)} %get-tuple-element.229, s32[]{:T(128)} %get-tuple-element.216), kind=kOutput, calls=%fused_computation.9.clone.1 | convolution fusion | flops 3526295552 | bytes 10879588 | tf_op jit(solution)/shard_map/while/body/eval_jaxpr/eyxrc,yxrk->eck/dot_general | solution.py:100
  161.4 0.6 dynamic_slice.59
  164.0 1.4 copy_bitcast_fusion.2
  165.4 8.9 %fusion.75 = f32[3,4,128,640]{3,2,1,0:T(8,128)} fusion(f32[3,4,128,640]{3,2,1,0:T(8,128)} %get-tuple-element.217, s32[]{:T(128)S(6)} %select_n.30, bf16[4,12]{1,0:T(4,128)(2,1)S(1)} %fusion.74, bf16[7,12,64,128]{3,2,0,1:T(8,128)(2,1)S(1)} %copy_bitcast_fusion.2, bf16[4,7,12,64,640]{4,3,2,1,0:T(8,128)(2,1)} %get-tuple-element.229, s32[]{:T(128)} %get-tuple-element.216), kind=kOutput, calls=%fused_computation.9.clone.1 | convolution fusion | flops 3526295552 | bytes 10879588 | tf_op jit(solution)/shard_map/while/body/eval_jaxpr/eyxrc,yxrk->eck/dot_general | solution.py:100
  174.4 0.6 dynamic_slice.59
  176.9 1.4 copy_bitcast_fusion.2
  178.4 9.0 %fusion.75 = f32[3,4,128,640]{3,2,1,0:T(8,128)} fusion(f32[3,4,128,640]{3,2,1,0:T(8,128)} %get-tuple-element.217, s32[]{:T(128)S(6)} %select_n.30, bf16[4,12]{1,0:T(4,128)(2,1)S(1)} %fusion.74, bf16[7,12,64,128]{3,2,0,1:T(8,128)(2,1)S(1)} %copy_bitcast_fusion.2, bf16[4,7,12,64,640]{4,3,2,1,0:T(8,128)(2,1)} %get-tuple-element.229, s32[]{:T(128)} %get-tuple-element.216), kind=kOutput, calls=%fused_computation.9.clone.1 | convolution fusion | flops 3526295552 | bytes 10879588 | tf_op jit(solution)/shard_map/while/body/eval_jaxpr/eyxrc,yxrk->eck/dot_general | solution.py:100
  187.4 0.6 dynamic_slice.59
  189.9 1.4 copy_bitcast_fusion.2
  191.4 8.9 %fusion.75 = f32[3,4,128,640]{3,2,1,0:T(8,128)} fusion(f32[3,4,128,640]{3,2,1,0:T(8,128)} %get-tuple-element.217, s32[]{:T(128)S(6)} %select_n.30, bf16[4,12]{1,0:T(4,128)(2,1)S(1)} %fusion.74, bf16[7,12,64,128]{3,2,0,1:T(8,128)(2,1)S(1)} %copy_bitcast_fusion.2, bf16[4,7,12,64,640]{4,3,2,1,0:T(8,128)(2,1)} %get-tuple-element.229, s32[]{:T(128)} %get-tuple-element.216), kind=kOutput, calls=%fused_computation.9.clone.1 | convolution fusion | flops 3526295552 | bytes 10879588 | tf_op jit(solution)/shard_map/while/body/eval_jaxpr/eyxrc,yxrk->eck/dot_general | solution.py:100
  200.3 1.4 slice_bitcast_fusion
  201.7 1.9 collective-permute-start.4
  203.6 1.4 slice.152
  205.0 17.7 %collective-permute-done.4 = f32[4,128,640]{2,1,0:T(8,128)S(1)} collective-permute-done((f32[4,128,640]{2,1,0:T(8,128)S(1)}, f32[4,128,640]{2,1,0:T(8,128)S(1)}, u32[]{:S(2)}, u32[]{:S(2)}) %collective-permute-start.4) | collective-permute-done | bytes 1310752 | tf_op jit(solution)/shard_map/ppermute | solution.py:23
  222.7 1.4 fusion.60
  224.2 1.2 pad_maximum_fusion.8
  225.4 0.0 copy-done.1
  (8 shorter events, 0.0 us)
Async XLA Ops:
  0.0 10.6 %copy-start = (s32[4,4]{1,0:T(4,128)S(1)}, s32[4,4]{1,0:T(4,128)}, u32[]{:S(2)}) copy-start(s32[4,4]{1,0:T(4,128)} %param.9) | copy-start | bytes 196
  0.0 23.6 %slice-start = ((s8[5505024]{0:T(1024)(128)(4,1)}), s8[1310720]{0:T(1024)(128)(4,1)S(1)}, s32[]{:S(2)}) async-start(s8[5505024]{0:T(1024)(128)(4,1)} %bitcast.99), calls=%async_computation | async-start | bytes 2621440
  4.1 19.3 %collective-permute-start = (bf16[1,7,12,64,128]{4,3,2,1,0:T(8,128)(2,1)}, bf16[1,7,12,64,128]{4,3,2,1,0:T(8,128)(2,1)S(1)}, u32[]{:S(2)}, u32[]{:S(2)}) collective-permute-start(bf16[1,7,12,64,128]{4,3,2,1,0:T(8,128)(2,1)} %get-tuple-element.164), channel_id=1, source_target_pairs={{0,4},{4,8},{8,12},{12,16},{16,20},{20,24},{24,28},{28,32},{32,36}... | collective-permute-start | bytes 4128776 | tf_op jit(solution)/shard_map/ppermute | solution.py:12
  7.9 22.1 %collective-permute-start.1 = (bf16[1,7,12,64,128]{4,3,2,1,0:T(8,128)(2,1)}, bf16[1,7,12,64,128]{4,3,2,1,0:T(8,128)(2,1)}, u32[]{:S(2)}, u32[]{:S(2)}) collective-permute-start(bf16[1,7,12,64,128]{4,3,2,1,0:T(8,128)(2,1)} %get-tuple-element.165), channel_id=1, source_target_pairs={{4,0},{8,4},{12,8},{16,12},{20,16},{24,20},{28,24},{32,28},{36,32}... | collective-permute-start | bytes 4128776 | tf_op jit(solution)/shard_map/ppermute | solution.py:15
  11.1 12.5 %slice-start.1 = ((s8[5505024]{0:T(1024)(128)(4,1)}), s8[4194304]{0:T(1024)(128)(4,1)S(1)}, s32[]{:S(2)}) async-start(s8[5505024]{0:T(1024)(128)(4,1)} %bitcast.99), calls=%async_computation.1 | async-start | bytes 8388608
  32.7 22.6 %collective-permute-start.2 = (bf16[6,7,1,64,128]{4,3,2,1,0:T(8,128)(2,1)}, bf16[6,7,1,64,128]{4,3,2,1,0:T(8,128)(2,1)S(1)}, u32[]{:S(2)}, u32[]{:S(2)}) collective-permute-start(bf16[6,7,1,64,128]{4,3,2,1,0:T(8,128)(2,1)} %get-tuple-element.162), channel_id=1, source_target_pairs={{0,1},{1,2},{2,3},{4,5},{5,6},{6,7},{8,9},{9,10},{10,11},{12,13},{... | collective-permute-start | bytes 2064392 | tf_op jit(solution)/shard_map/ppermute | solution.py:12
  35.8 19.5 %collective-permute-start.3 = (bf16[6,7,1,64,128]{4,3,2,1,0:T(8,128)(2,1)}, bf16[6,7,1,64,128]{4,3,2,1,0:T(8,128)(2,1)}, u32[]{:S(2)}, u32[]{:S(2)}) collective-permute-start(bf16[6,7,1,64,128]{4,3,2,1,0:T(8,128)(2,1)} %get-tuple-element.163), channel_id=1, source_target_pairs={{1,0},{2,1},{3,2},{5,4},{6,5},{7,6},{9,8},{10,9},{11,10},{13,12},{... | collective-permute-start | bytes 2064392 | tf_op jit(solution)/shard_map/ppermute | solution.py:15
  124.8 17.1 %slice-start.2 = ((s8[11010048]{0:T(1024)(128)(4,1)}), s8[4194304]{0:T(1024)(128)(4,1)S(1)}, s32[]{:S(2)}) async-start(s8[11010048]{0:T(1024)(128)(4,1)} %bitcast.101), calls=%async_computation.2 | async-start | bytes 8388608
  124.8 17.1 %slice-start.3 = ((s8[11010048]{0:T(1024)(128)(4,1)}), s8[4194304]{0:T(1024)(128)(4,1)S(1)}, s32[]{:S(2)}) async-start(s8[11010048]{0:T(1024)(128)(4,1)} %bitcast.101), calls=%async_computation.3 | async-start | bytes 8388608
  133.3 8.5 %slice-start.4 = ((s8[11010048]{0:T(1024)(128)(4,1)}), s8[2621440]{0:T(1024)(128)(4,1)S(1)}, s32[]{:S(2)}) async-start(s8[11010048]{0:T(1024)(128)(4,1)} %bitcast.101), calls=%async_computation.4 | async-start | bytes 5242880
  200.3 25.1 %copy-start.1 = (s32[4,4]{1,0:T(4,128)S(1)}, s32[4,4]{1,0:T(4,128)}, u32[]{:S(2)}) copy-start(s32[4,4]{1,0:T(4,128)} %param.9) | copy-start | bytes 196
  201.7 21.0 %collective-permute-start.4 = (f32[4,128,640]{2,1,0:T(8,128)S(1)}, f32[4,128,640]{2,1,0:T(8,128)S(1)}, u32[]{:S(2)}, u32[]{:S(2)}) collective-permute-start(f32[4,128,640]{2,1,0:T(8,128)S(1)} %slice_bitcast_fusion), channel_id=1, source_target_pairs={{4,0},{8,4},{12,8},{16,12},{20,16},{24,20},{28,24},{32,28},{36,32}... | collective-permute-start | bytes 3932168 | tf_op jit(solution)/shard_map/ppermute | solution.py:23
where the time goes:
time: 227 us; the launch traced here: 225 us
  matrix products  117 us (52%)
  other arithmetic  39.7 us (17%)
  waiting for transfers between devices  24.3 us (11%)
  local copies, waits for them, and re-layouts  23.1 us (10%)
  starting transfers between devices  13.1 us (6%)
  loops' own time  7.83 us (3%)
    dot_general x7, matrix products, neighbour_products(): jnp.einsum('zyxrs,zyxsc->zyxrc', a_blocks[..., k * width:(k + 1) * width]...  81.4 us
    dot_general x4, matrix products, accumulate(): jnp.einsum('eyxrc,yxrk->eck', masked, slots, preferred_element_type=jnp.f...  35.8 us
    unnamed x5, other arithmetic  25.5 us
    ppermute x1, waiting for transfers between devices, passed_along(): return lax.ppermute(block, axis, route)  17.7 us
    another operation x1, loops' own time, per_device(): running = lax.fori_loop(0, layers, accumulate, start)  7.83 us
    ppermute x2, starting transfers between devices, with_halo(): lax.ppermute(lax.slice_in_dim(block, block.shape[dim] - width, None, axis...  6.86 us
    concatenate x1, other arithmetic, with_halo(): block = jnp.concatenate([low, block, high], axis=dim)  6.77 us
    mul x4, local copies, waits for them, and re-layouts, accumulate(): masked = piece[None] * member[:, None, :, None, None]  5.78 us
  transfers between devices with their start and end apart: 5, of which 3 were waited for; matrix products, arithmetic and copies ran while one was open for 14% of the time, Pallas kernels for 0%

commit v1 on v0

v1 whole, which is shorter than its diff:
```python
import functools

import jax
import jax.numpy as jnp
from jax import lax
from jax.experimental import pallas as pl
from jax.experimental.pallas import tpu as pltpu
from jax.sharding import PartitionSpec as P

BF = jnp.bfloat16
F32 = jnp.float32
UNROLL = 4


def product(lhs, rhs):
    return jnp.dot(lhs, rhs, preferred_element_type=F32)


def kernel(
    n_dom, n_grp, zagg, xlen, a_hbm, p_hbm, out_hbm,
    a, p, pt, rt, ert, v, ev, xv, below, above, left, right,
    carry_out, carry_in, last, done,
    a_sem, p_sem, z_send, z_recv, x_send, x_recv, c_send, c_recv, o_sem,
):
    layers, depth, columns, block, width = p.shape
    chunk = columns // 3
    intervals = xlen.shape[1]
    dom, grp = lax.axis_index("dom"), lax.axis_index("grp")
    has_below, has_above = dom > 0, dom < n_dom - 1
    has_left, has_right = grp > 0, grp < n_grp - 1
    MESH = pl.DeviceIdType.MESH
    sides = (
        (has_below, (dom - 1, grp)),
        (has_above, (dom + 1, grp)),
        (has_left, (dom, grp - 1)),
        (has_right, (dom, grp + 1)),
    )

    def part(ref, z, third):
        return ref.at[z, :, pl.ds(third * chunk, chunk)]

    a_copies = [
        [pltpu.make_async_copy(part(a_hbm, z, t), part(a, z, t), a_sem.at[z, t]) for t in range(3)]
        for z in range(layers)
    ]
    p_copies = [pltpu.make_async_copy(p_hbm.at[z], p.at[z], p_sem.at[z]) for z in range(layers)]
    p_copies[0].start()
    a_copies[0][0].start()
    p_copies[1].start()
    a_copies[0][1].start()
    a_copies[0][2].start()
    for z in range(1, layers):
        if z + 1 < layers:
            p_copies[z + 1].start()
        for t in range(3):
            a_copies[z][t].start()

    barrier = pltpu.get_barrier_semaphore()
    for there, device in sides:
        @pl.when(there)
        def _(device=device):
            pl.semaphore_signal(barrier, inc=1, device_id=device, device_id_type=MESH)
    pl.semaphore_wait(barrier, sum(jnp.where(there, 1, 0).astype(jnp.int32) for there, _ in sides))

    def remote(src, dst, send, recv, device):
        return pltpu.make_async_remote_copy(
            src_ref=src, dst_ref=dst, send_sem=send, recv_sem=recv,
            device_id=device, device_id_type=MESH,
        )

    def thirds(ref, t):
        return ref.at[:, pl.ds(t * chunk, chunk)]

    up = [
        remote(part(p_hbm, layers - 1, t), thirds(below, t), z_send.at[0, t], z_recv.at[0, t], (dom + 1, grp))
        for t in range(3)
    ]
    down = [
        remote(part(p_hbm, 0, t), thirds(above, t), z_send.at[1, t], z_recv.at[1, t], (dom - 1, grp))
        for t in range(3)
    ]
    rightward = remote(p_hbm.at[:, :, columns - 1], left, x_send.at[0], x_recv.at[0], (dom, grp + 1))
    leftward = remote(p_hbm.at[:, :, 0], right, x_send.at[1], x_recv.at[1], (dom, grp - 1))
    carry = remote(carry_out, carry_in, c_send, c_recv, (dom - 1, grp))

    @pl.when(has_above)
    def _():
        for t in range(3):
            up[t].start()

    @pl.when(has_below)
    def _():
        for t in range(3):
            down[t].start()

    @pl.when(has_right)
    def _():
        rightward.start()

    @pl.when(has_left)
    def _():
        leftward.start()

    for there, ref in ((has_below, below), (has_above, above), (has_left, left), (has_right, right), (has_above, carry_in)):
        @pl.when(jnp.logical_not(there))
        def _(ref=ref):
            for first in range(ref.shape[0]):
                ref[first] = jnp.zeros(ref.shape[1:], ref.dtype)

    one, none = jnp.int32(1), jnp.int32(0)

    def begins_at(layer):
        at = dom * layers + layer
        inner = jnp.where(
            zagg[jnp.minimum(at, n_dom * layers - 1)] != zagg[jnp.maximum(at - 1, 0)], one, none
        )
        return jnp.where(jnp.logical_or(at == 0, at == n_dom * layers), one, inner)

    begins = [begins_at(layer) for layer in range(layers + 1)]
    group = [begins[0]]
    for layer in range(1, layers):
        group.append(group[-1] + begins[layer])
    cuts = [none]
    for i in range(intervals):
        cuts.append(cuts[-1] + xlen[grp, i])

    def column_begins(x):
        found = none
        for i in range(intervals):
            found = jnp.where(x == cuts[i], one, found)
        return jnp.where(x == columns, one, found)

    def real(flag):
        return flag.astype(F32)

    rows = [slice(y * block, (y + 1) * block) for y in range(depth)]

    def main(z):
        low, high = z > 0, z < layers - 1
        slots = width * (1 + low + high)

        def first(x, slot):
            same_xm = (1.0 - real(column_begins(x))).astype(BF)
            same_xp = (1.0 - real(column_begins(x + 1))).astype(BF)
            xm, xp = jnp.maximum(x - 1, 0), jnp.minimum(x + 1, columns - 1)
            zero = jnp.zeros((block, width), BF)
            for y in range(depth):
                stack = jnp.concatenate(
                    [
                        p[z, y, x],
                        p[z, y, xm] * same_xm,
                        p[z, y, xp] * same_xp,
                        p[z, y - 1, x] if y > 0 else zero,
                        p[z, y + 1, x] if y < depth - 1 else zero,
                    ],
                    axis=0,
                )
                rt[slot, rows[y], 0:width] = product(a[z, y, x, :, 0 : 5 * block], stack).astype(BF)
                at = width
                if high:
                    rt[slot, rows[y], at : at + width] = product(
                        a[z, y, x, :, 6 * block : 7 * block], p[z + 1, y, x]
                    ).astype(BF)
                    at += width
                if low:
                    rt[slot, rows[y], at : at + width] = product(
                        a[z, y, x, :, 5 * block : 6 * block], p[z - 1, y, x]
                    ).astype(BF)

        def second(x, slot):
            turned = jnp.concatenate([p[z, y, x] for y in range(depth)], axis=0).T
            pt[z, x] = turned
            coarse = product(turned, rt[slot, :, 0:slots])
            before = v[z, jnp.maximum(x - 1, 0), :, 0:slots]
            v[z, x, :, 0:slots] = coarse + jnp.where(column_begins(x) == 1, 0.0, before)

        def step(j, _):
            for u in range(UNROLL):
                first(j * UNROLL + u, u)
                if u > 0:
                    second(j * UNROLL + u - 1, u - 1)
            second(j * UNROLL + UNROLL - 1, UNROLL - 1)
            return 0

        lax.fori_loop(0, columns // UNROLL, step, 0)

    def inside_columns(z):
        for i in range(1, intervals):
            hi = jnp.clip(cuts[i], 1, columns - 1)
            lo = hi - 1
            for y in range(depth):
                ert[0, rows[y]] = product(a[z, y, lo, :, 2 * block : 3 * block], p[z, y, hi]).astype(BF)
                ert[1, rows[y]] = product(a[z, y, hi, :, block : 2 * block], p[z, y, lo]).astype(BF)
            xv[1, z, i - 1] = product(pt[z, lo], ert[0])
            xv[0, z, i] = product(pt[z, hi], ert[1])

    def outer_columns(z):
        for y in range(depth):
            ert[2, rows[y]] = product(a[z, y, columns - 1, :, 2 * block : 3 * block], right[z, y]).astype(BF)
            ert[3, rows[y]] = product(a[z, y, 0, :, block : 2 * block], left[z, y]).astype(BF)
        xv[1, z, intervals - 1] = product(pt[z, columns - 1], ert[2])
        xv[0, z, 0] = product(pt[z, 0], ert[3])

    def x_sides(z):
        inside_columns(z)
        outer_columns(z)

    def outer_layer(side, z, k, ref, t):
        def step(j, _):
            for u in range(chunk):
                x = t * chunk + j * chunk + u
                for y in range(depth):
                    ert[u, rows[y]] = product(a[z, y, x, :, k * block : (k + 1) * block], ref[y, x]).astype(BF)
                coarse = product(pt[z, x], ert[u])
                before = ev[side, jnp.maximum(x - 1, 0)]
                ev[side, x] = coarse + jnp.where(column_begins(x) == 1, 0.0, before)
            return 0

        lax.fori_loop(0, 1, step, 0)

    S = [slice(k * width, (k + 1) * width) for k in range(5)]

    def layer_slots(z, i):
        end = jnp.clip(cuts[i + 1] - 1, 0, columns - 1)
        own = v[z, end, :, S[0]]
        zp = v[z, end, :, S[1]] if z < layers - 1 else ev[1, end]
        zm = v[z, end, :, S[2] if z < layers - 1 else S[1]] if z > 0 else ev[0, end]
        here, there = real(begins[z]), real(begins[z + 1])
        own = own + (1.0 - here) * zm + (1.0 - there) * zp
        return own, xv[0, z, i], xv[1, z, i], here * zm, there * zp

    def gathered(i, zs, wanted, slots):
        total = None
        for z in zs:
            w = real(jnp.where(group[z] == wanted, one, none))
            terms = layer_slots(z, i)
            terms = [terms[s] * w for s in slots]
            total = terms if total is None else [t + u for t, u in zip(total, terms)]
        return total

    p_copies[0].wait()
    for z in range(layers - 1):
        p_copies[z + 1].wait()
        for t in range(3):
            a_copies[z][t].wait()
        main(z)
    for t in range(3):
        a_copies[layers - 1][t].wait()

    @pl.when(has_left)
    def _():
        rightward.wait_recv()

    @pl.when(has_right)
    def _():
        leftward.wait_recv()

    for z in range(2):
        x_sides(z)
    for t in range(3):
        @pl.when(has_below)
        def _(t=t):
            up[t].wait_recv()
        outer_layer(0, 0, 5, below, t)
    for i in range(intervals):
        for s, term in enumerate(gathered(i, (0, 1), 0, (0, 1, 2, 4))):
            carry_out[i, :, S[s]] = term.astype(BF)

    @pl.when(has_below)
    def _():
        carry.start()

    main(layers - 1)
    for z in range(2, layers):
        x_sides(z)
    for i in range(intervals):
        for s, term in enumerate(gathered(i, range(layers - 1), 1, range(5))):
            done[0, i, :, S[s]] = term.astype(BF)
    first_out = pltpu.make_async_copy(done.at[0], out_hbm.at[0], o_sem.at[0])
    first_out.start()
    for t in range(3):
        @pl.when(has_above)
        def _(t=t):
            down[t].wait_recv()
        outer_layer(1, layers - 1, 6, above, t)
    for i in range(intervals):
        for s, term in enumerate(gathered(i, range(1, layers), 2, range(5))):
            last[i, :, S[s]] = term

    @pl.when(has_above)
    def _():
        carry.wait_recv()

    for i in range(intervals):
        for s, c in ((0, 0), (1, 1), (2, 2), (4, 3)):
            done[1, i, :, S[s]] = (last[i, :, S[s]] + carry_in[i, :, S[c]].astype(F32)).astype(BF)
        done[1, i, :, S[3]] = last[i, :, S[3]].astype(BF)
    second_out = pltpu.make_async_copy(done.at[1], out_hbm.at[1], o_sem.at[1])
    second_out.start()

    @pl.when(has_above)
    def _():
        for t in range(3):
            up[t].wait_send()

    @pl.when(has_below)
    def _():
        for t in range(3):
            down[t].wait_send()
        carry.wait_send()

    @pl.when(has_right)
    def _():
        rightward.wait_send()

    @pl.when(has_left)
    def _():
        leftward.wait_send()

    first_out.wait()
    second_out.wait()


def per_device(n_dom, n_grp, a_blocks, prolong, zagg, xlen):
    layers, depth, columns, block, width = prolong.shape
    intervals = xlen.shape[1]
    long = depth * block
    vm, dma = pltpu.VMEM, pltpu.SemaphoreType.DMA
    return pl.pallas_call(
        functools.partial(kernel, n_dom, n_grp),
        out_shape=jax.ShapeDtypeStruct((layers // 2, intervals, width, 5 * width), BF),
        in_specs=[pl.BlockSpec(memory_space=pltpu.SMEM)] * 2 + [pl.BlockSpec(memory_space=pl.ANY)] * 2,
        out_specs=pl.BlockSpec(memory_space=pl.ANY),
        scratch_shapes=[
            vm(a_blocks.shape, BF),
            vm(prolong.shape, BF),
            vm((layers, columns, width, long), BF),
            vm((UNROLL, long, 3 * width), BF),
            vm((4, long, width), BF),
            vm((layers, columns, width, 3 * width), F32),
            vm((2, columns, width, width), F32),
            vm((2, layers, intervals, width, width), F32),
            vm(prolong.shape[1:], BF),
            vm(prolong.shape[1:], BF),
            vm((layers, depth, block, width), BF),
            vm((layers, depth, block, width), BF),
            vm((intervals, width, 4 * width), BF),
            vm((intervals, width, 4 * width), BF),
            vm((intervals, width, 5 * width), F32),
            vm((layers // 2, intervals, width, 5 * width), BF),
            dma((layers, 3)), dma((layers,)), dma((2, 3)), dma((2, 3)),
            dma((2,)), dma((2,)), dma, dma, dma((2,)),
        ],
        compiler_params=pltpu.CompilerParams(
            collective_id=0, has_side_effects=True, vmem_limit_bytes=62 * 2**20
        ),
    )(zagg, xlen, a_blocks, prolong)


def solution(mesh):
    in_specs = (P("dom", None, "grp", None, None), P("dom", None, "grp", None, None), P(), P())
    return jax.shard_map(
        functools.partial(per_device, mesh.shape["dom"], mesh.shape["grp"]),
        mesh=mesh, in_specs=in_specs, out_specs=P("dom", "grp", None, None), check_vma=False,
    )
```

time: 227 us -> 37.3 us (0.16)
  matrix products: 117 us -> 0 us
  other arithmetic: 39.7 us -> 0 us
  Pallas kernels: 0 us -> 34.3 us
  waiting for transfers between devices: 24.3 us -> 0 us
  local copies, waits for them, and re-layouts: 23.1 us -> 2.51 us
  starting transfers between devices: 13.1 us -> 0 us
  loops' own time: 7.83 us -> 0 us
    dot_general x11 -> x0, matrix products: 117 us -> none  [the longest x7 81.4 us: neighbour_products(): jnp.einsum('zyxrs,zyxsc->zyxrc', a_blocks[..., k * width:(k + 1) * width]...]
    pallas_call x0 -> x1, Pallas kernels: none -> 34.3 us  [per_device(): pl.pallas_call(functools.partial(kernel, n_dom, n_grp), out_shape=jax.Sha...]
    unnamed x5 -> x0, other arithmetic: 25.5 us -> none
    ppermute x5 -> x0, waiting for transfers between devices: 24.3 us -> none  [the longest x1 17.7 us: passed_along(): return lax.ppermute(block, axis, route)]
    ppermute x5 -> x0, starting transfers between devices: 13.1 us -> none  [the longest x2 6.86 us: with_halo(): lax.ppermute(lax.slice_in_dim(block, block.shape[dim] - width, None, axis...]
    concatenate x3 -> x0, other arithmetic: 12.3 us -> none  [the longest x1 6.77 us: with_halo(): block = jnp.concatenate([low, block, high], axis=dim)]
    another operation x1 -> x0, loops' own time: 7.83 us -> none  [per_device(): running = lax.fori_loop(0, layers, accumulate, start)]
    slice x3 -> x0, local copies, waits for them, and re-layouts: 6.71 us -> none  [the longest x2 5.32 us: with_halo(): lax.slice_in_dim(block, block.shape[dim] - width, None, axis=dim)]
  transfers between devices with their start and end apart: 5 -> 0, of which waited for: 3 -> 0; matrix products, arithmetic and copies ran while one was open for 14% -> 0% of each run, Pallas kernels for 0% -> 0%
where the time goes in v1:
time: 37.3 us; the launch traced here: 36.8 us
  Pallas kernels  34.3 us (92%)
  local copies, waits for them, and re-layouts  2.51 us (7%)
    pallas_call x1, Pallas kernels, per_device(): pl.pallas_call(functools.partial(kernel, n_dom, n_grp), out_shape=jax.Sha...  34.3 us
    unnamed x1, local copies, waits for them, and re-layouts  2.51 us

profile of v1, /device:TPU:27, one launch (start us, length us, event | category | flops | bytes accessed | tf_op | source)
XLA Modules:
  0.0 36.8 jit_solution(9250223628589034130)
XLA Ops:
  0.0 34.3 %shard_map.46 = bf16[2,4,128,640]{3,2,1,0:T(8,128)(2,1)} custom-call(s32[128]{0:T(128)} %zagg.1, s32[4,4]{1,0:T(4,128)} %xlen.1, bf16[4,7,12,64,448]{4,3,2,1,0:T(8,128)(2,1)} %a_hbm.1, bf16[4,7,12,64,128]{4,3,2,1,0:T(8,128)(2,1)} %p_hbm.1), custom_call_target="tpu_custom_call" | custom-call | tf_op jit(solution)/shard_map/pallas_call | solution.py:329
  34.3 2.5 %copy.6 = bf16[2,4,128,640]{3,2,1,0:T(8,128)(2,1)} copy(bf16[2,4,128,640]{3,2,1,0:T(8,128)(2,1)} %shard_map.46) | data formatting | bytes 2621440

commit v2 on v1

v2 whole, which is shorter than its diff:
```python
import functools

import jax
import jax.numpy as jnp
from jax import lax
from jax.experimental import pallas as pl
from jax.experimental.pallas import tpu as pltpu
from jax.sharding import PartitionSpec as P

BF = jnp.bfloat16
F32 = jnp.float32
UNROLL = 4


def product(lhs, rhs):
    return jnp.dot(lhs, rhs, preferred_element_type=F32)


def kernel(
    n_dom, n_grp, zagg, xlen, a_hbm, p_hbm, done,
    a, p, pt, rt, ert, v, xv, below, above, left, right,
    carry_out, carry_in, last,
    a_sem, p_sem, z_send, z_recv, x_send, x_recv, c_send, c_recv,
):
    layers, depth, columns, block, width = p.shape
    chunk = columns // 3
    intervals = xlen.shape[1]
    dom, grp = lax.axis_index("dom"), lax.axis_index("grp")
    has_below, has_above = dom > 0, dom < n_dom - 1
    has_left, has_right = grp > 0, grp < n_grp - 1
    MESH = pl.DeviceIdType.MESH
    sides = (
        (has_below, (dom - 1, grp)),
        (has_above, (dom + 1, grp)),
        (has_left, (dom, grp - 1)),
        (has_right, (dom, grp + 1)),
    )

    def part(ref, z, third):
        return ref.at[z, :, pl.ds(third * chunk, chunk)]

    def a_copy(z, t):
        return pltpu.make_async_copy(part(a_hbm, z, t), part(a, z, t), a_sem.at[z, t])

    def p_copy(z, h):
        half = pl.ds(h * (columns // 2), columns // 2)
        return pltpu.make_async_copy(p_hbm.at[z, :, half], p.at[z, :, half], p_sem.at[z, h])

    order = [*range(1, layers - 1), 0, layers - 1]
    for z in range(3):
        p_copy(z, 0).start()
    a_copy(1, 0).start()
    for z in range(3):
        p_copy(z, 1).start()
    a_copy(1, 1).start()
    a_copy(1, 2).start()
    for z in range(3, layers):
        p_copy(z, 0).start()
        p_copy(z, 1).start()
    for z in order[1:]:
        for t in range(3):
            a_copy(z, t).start()

    barrier = pltpu.get_barrier_semaphore()
    for there, device in sides:
        @pl.when(there)
        def _(device=device):
            pl.semaphore_signal(barrier, inc=1, device_id=device, device_id_type=MESH)
    pl.semaphore_wait(barrier, sum(jnp.where(there, 1, 0).astype(jnp.int32) for there, _ in sides))

    def remote(src, dst, send, recv, device):
        return pltpu.make_async_remote_copy(
            src_ref=src, dst_ref=dst, send_sem=send, recv_sem=recv,
            device_id=device, device_id_type=MESH,
        )

    def thirds(ref, t):
        return ref.at[:, pl.ds(t * chunk, chunk)]

    def up_third(t):
        return remote(part(p_hbm, layers - 1, t), thirds(below, t), z_send.at[0, t], z_recv.at[0, t], (dom + 1, grp))

    def down_third(t):
        return remote(part(p_hbm, 0, t), thirds(above, t), z_send.at[1, t], z_recv.at[1, t], (dom - 1, grp))

    rightward = remote(p_hbm.at[:, :, columns - 1], left, x_send.at[0], x_recv.at[0], (dom, grp + 1))
    leftward = remote(p_hbm.at[:, :, 0], right, x_send.at[1], x_recv.at[1], (dom, grp - 1))
    carry = remote(carry_out, carry_in, c_send, c_recv, (dom - 1, grp))

    @pl.when(has_above)
    def _():
        for t in range(3):
            up_third(t).start()

    @pl.when(has_below)
    def _():
        for t in range(3):
            down_third(t).start()

    @pl.when(has_right)
    def _():
        rightward.start()

    @pl.when(has_left)
    def _():
        leftward.start()

    for there, ref in ((has_below, below), (has_above, above), (has_left, left), (has_right, right), (has_above, carry_in)):
        @pl.when(jnp.logical_not(there))
        def _(ref=ref):
            for first in range(ref.shape[0]):
                ref[first] = jnp.zeros(ref.shape[1:], ref.dtype)

    one, none = jnp.int32(1), jnp.int32(0)

    def begins_at(layer):
        at = dom * layers + layer
        inner = jnp.where(
            zagg[jnp.minimum(at, n_dom * layers - 1)] != zagg[jnp.maximum(at - 1, 0)], one, none
        )
        return jnp.where(jnp.logical_or(at == 0, at == n_dom * layers), one, inner)

    begins = [begins_at(layer) for layer in range(layers + 1)]
    group = [begins[0]]
    for layer in range(1, layers):
        group.append(group[-1] + begins[layer])
    cuts = [none]
    for i in range(intervals):
        cuts.append(cuts[-1] + xlen[grp, i])

    def column_begins(x):
        found = none
        for i in range(intervals):
            found = jnp.where(x == cuts[i], one, found)
        return jnp.where(x == columns, one, found)

    def real(flag):
        return flag.astype(F32)

    rows = [slice(y * block, (y + 1) * block) for y in range(depth)]

    def main(z):
        slots = 3 * width

        def over(y, x):
            return p[z + 1, y, x] if z < layers - 1 else above[y, x]

        def under(y, x):
            return p[z - 1, y, x] if z > 0 else below[y, x]

        def first(x, slot):
            same_xm = (1.0 - real(column_begins(x))).astype(BF)
            same_xp = (1.0 - real(column_begins(x + 1))).astype(BF)
            xm, xp = jnp.maximum(x - 1, 0), jnp.minimum(x + 1, columns - 1)
            zero = jnp.zeros((block, width), BF)
            for y in range(depth):
                stack = jnp.concatenate(
                    [
                        p[z, y, x],
                        p[z, y, xm] * same_xm,
                        p[z, y, xp] * same_xp,
                        p[z, y - 1, x] if y > 0 else zero,
                        p[z, y + 1, x] if y < depth - 1 else zero,
                    ],
                    axis=0,
                )
                rt[slot, rows[y], 0:width] = product(a[z, y, x, :, 0 : 5 * block], stack).astype(BF)
                rt[slot, rows[y], width : 2 * width] = product(
                    a[z, y, x, :, 6 * block : 7 * block], over(y, x)
                ).astype(BF)
                rt[slot, rows[y], 2 * width : slots] = product(
                    a[z, y, x, :, 5 * block : 6 * block], under(y, x)
                ).astype(BF)

        def second(x, slot):
            turned = jnp.concatenate([p[z, y, x] for y in range(depth)], axis=0).T
            pt[z, x] = turned
            coarse = product(turned, rt[slot, :, 0:slots])
            before = v[z, jnp.maximum(x - 1, 0), :, 0:slots]
            v[z, x, :, 0:slots] = coarse + jnp.where(column_begins(x) == 1, 0.0, before)

        def step(j, _):
            if z in order[:-2]:
                a_copy(z, j).wait()
            if z == order[0]:
                @pl.when(j == 1)
                def _():
                    for other in range(3):
                        p_copy(other, 1).wait()
            if z == 0:
                @pl.when(has_below)
                def _():
                    up_third(j).wait_recv()
            if z == layers - 1:
                @pl.when(has_above)
                def _():
                    down_third(j).wait_recv()
            for u in range(UNROLL):
                first(j * UNROLL + u, u)
                if u > 0:
                    second(j * UNROLL + u - 1, u - 1)
            second(j * UNROLL + UNROLL - 1, UNROLL - 1)
            return 0

        lax.fori_loop(0, columns // UNROLL, step, 0)

    def x_sides(z, at):
        for i in range(1, intervals):
            hi = jnp.clip(cuts[i], 1, columns - 1)
            lo = hi - 1
            for y in range(depth):
                ert[at, rows[y]] = product(a[z, y, lo, :, 2 * block : 3 * block], p[z, y, hi]).astype(BF)
                ert[at + 1, rows[y]] = product(a[z, y, hi, :, block : 2 * block], p[z, y, lo]).astype(BF)
            xv[1, z, i - 1] = product(pt[z, lo], ert[at])
            xv[0, z, i] = product(pt[z, hi], ert[at + 1])
            at += 2
        for y in range(depth):
            ert[at, rows[y]] = product(a[z, y, columns - 1, :, 2 * block : 3 * block], right[z, y]).astype(BF)
            ert[at + 1, rows[y]] = product(a[z, y, 0, :, block : 2 * block], left[z, y]).astype(BF)
        xv[1, z, intervals - 1] = product(pt[z, columns - 1], ert[at])
        xv[0, z, 0] = product(pt[z, 0], ert[at + 1])

    S = [slice(k * width, (k + 1) * width) for k in range(5)]

    def layer_slots(z, i):
        end = jnp.clip(cuts[i + 1] - 1, 0, columns - 1)
        own = v[z, end, :, S[0]]
        zp, zm = v[z, end, :, S[1]], v[z, end, :, S[2]]
        here, there = real(begins[z]), real(begins[z + 1])
        own = own + (1.0 - here) * zm + (1.0 - there) * zp
        return own, xv[0, z, i], xv[1, z, i], here * zm, there * zp

    def gathered(i, zs, wanted, slots):
        total = None
        for z in zs:
            w = real(jnp.where(group[z] == wanted, one, none))
            terms = layer_slots(z, i)
            terms = [terms[s] * w for s in slots]
            total = terms if total is None else [t + u for t, u in zip(total, terms)]
        return total

    for z in range(3):
        p_copy(z, 0).wait()
    main(1)
    for z in range(3, layers):
        p_copy(z, 0).wait()
        p_copy(z, 1).wait()
    for z in order[1:-2]:
        main(z)

    @pl.when(has_left)
    def _():
        rightward.wait_recv()

    @pl.when(has_right)
    def _():
        leftward.wait_recv()

    for t in range(3):
        a_copy(0, t).wait()
        a_copy(layers - 1, t).wait()
    for n, z in enumerate(order[:-2]):
        x_sides(z, 2 * intervals * n)
    main(0)
    x_sides(0, 0)
    for i in range(intervals):
        for s, term in enumerate(gathered(i, (0, 1), 0, (0, 1, 2, 4))):
            carry_out[i, :, S[s]] = term.astype(BF)

    @pl.when(has_below)
    def _():
        carry.start()

    main(layers - 1)
    x_sides(layers - 1, 0)
    for i in range(intervals):
        for s, term in enumerate(gathered(i, range(layers - 1), 1, range(5))):
            done[0, i, :, S[s]] = term.astype(BF)
    for i in range(intervals):
        for s, term in enumerate(gathered(i, range(1, layers), 2, range(5))):
            last[i, :, S[s]] = term

    @pl.when(has_above)
    def _():
        carry.wait_recv()

    for i in range(intervals):
        for s, c in ((0, 0), (1, 1), (2, 2), (4, 3)):
            done[1, i, :, S[s]] = (last[i, :, S[s]] + carry_in[i, :, S[c]].astype(F32)).astype(BF)
        done[1, i, :, S[3]] = last[i, :, S[3]].astype(BF)

    @pl.when(has_above)
    def _():
        for t in range(3):
            up_third(t).wait_send()

    @pl.when(has_below)
    def _():
        for t in range(3):
            down_third(t).wait_send()
        carry.wait_send()

    @pl.when(has_right)
    def _():
        rightward.wait_send()

    @pl.when(has_left)
    def _():
        leftward.wait_send()


def settle(made, out, sem):
    copies = [pltpu.make_async_copy(made.at[j, i], out.at[j, i], sem.at[j, i]) for j in range(2) for i in range(4)]
    for copy in copies:
        copy.start()
    for copy in copies:
        copy.wait()


def per_device(n_dom, n_grp, a_blocks, prolong, zagg, xlen):
    layers, depth, columns, block, width = prolong.shape
    intervals = xlen.shape[1]
    long = depth * block
    vm, dma = pltpu.VMEM, pltpu.SemaphoreType.DMA
    made = pl.pallas_call(
        functools.partial(kernel, n_dom, n_grp),
        out_shape=vm((layers // 2, intervals, width, 5 * width), BF),
        in_specs=[pl.BlockSpec(memory_space=pltpu.SMEM)] * 2 + [pl.BlockSpec(memory_space=pl.ANY)] * 2,
        out_specs=pl.BlockSpec(memory_space=pltpu.VMEM),
        scratch_shapes=[
            vm(a_blocks.shape, BF),
            vm(prolong.shape, BF),
            vm((layers, columns, width, long), BF),
            vm((UNROLL, long, 3 * width), BF),
            vm((4 * intervals, long, width), BF),
            vm((layers, columns, width, 3 * width), F32),
            vm((2, layers, intervals, width, width), F32),
            vm(prolong.shape[1:], BF),
            vm(prolong.shape[1:], BF),
            vm((layers, depth, block, width), BF),
            vm((layers, depth, block, width), BF),
            vm((intervals, width, 4 * width), BF),
            vm((intervals, width, 4 * width), BF),
            vm((intervals, width, 5 * width), F32),
            dma((layers, 3)), dma((layers, 2)), dma((2, 3)), dma((2, 3)),
            dma((2,)), dma((2,)), dma, dma,
        ],
        compiler_params=pltpu.CompilerParams(
            collective_id=0, has_side_effects=True, vmem_limit_bytes=60 * 2**20
        ),
    )(zagg, xlen, a_blocks, prolong)
    return pl.pallas_call(
        settle,
        out_shape=jax.ShapeDtypeStruct(made.shape, BF),
        in_specs=[pl.BlockSpec(memory_space=pl.ANY)],
        out_specs=pl.BlockSpec(memory_space=pl.ANY),
        scratch_shapes=[dma((2, 4))],
        compiler_params=pltpu.CompilerParams(vmem_limit_bytes=2**20),
    )(made)


def solution(mesh):
    in_specs = (P("dom", None, "grp", None, None), P("dom", None, "grp", None, None), P(), P())
    return jax.shard_map(
        functools.partial(per_device, mesh.shape["dom"], mesh.shape["grp"]),
        mesh=mesh, in_specs=in_specs, out_specs=P("dom", "grp", None, None), check_vma=False,
    )
```

time: 37.3 us -> 33.9 us (0.909)
  local copies, waits for them, and re-layouts: 2.51 us -> 0 us
  Pallas kernels: 34.3 us -> 33.8 us
    unnamed x1 -> x0, local copies, waits for them, and re-layouts: 2.51 us -> none
    pallas_call x1 -> x2, Pallas kernels: 34.3 us -> 33.8 us  [the longest x1 32.6 us: per_device(): pl.pallas_call(functools.partial(kernel, n_dom, n_grp), out_shape=vm((lay...]
where the time goes in v2:
time: 33.9 us; the launch traced here: 33.8 us
  Pallas kernels  33.8 us (100%)
    pallas_call x1, Pallas kernels, per_device(): pl.pallas_call(functools.partial(kernel, n_dom, n_grp), out_shape=vm((lay...  32.6 us
    pallas_call x1, Pallas kernels, per_device(): pl.pallas_call(settle, out_shape=jax.ShapeDtypeStruct(made.shape, BF), in...  1.12 us

profile of v2, /device:TPU:27, one launch (start us, length us, event | category | flops | bytes accessed | tf_op | source)
XLA Modules:
  0.0 33.8 jit_solution(9755407151365396846)
XLA Ops:
  0.0 32.6 %shard_map.46.made = bf16[2,4,128,640]{3,2,1,0:T(8,128)(2,1)S(1)} custom-call(s32[128]{0:T(128)} %zagg.1, s32[4,4]{1,0:T(4,128)} %xlen.1, bf16[4,7,12,64,448]{4,3,2,1,0:T(8,128)(2,1)} %a_hbm.1, bf16[4,7,12,64,128]{4,3,2,1,0:T(8,128)(2,1)} %p_hbm.1), custom_call_target="tpu_custom_call" | custom-call | tf_op jit(solution)/shard_map/pallas_call | solution.py:325
  32.7 1.1 %shard_map.47 = bf16[2,4,128,640]{3,2,1,0:T(8,128)(2,1)} custom-call(bf16[2,4,128,640]{3,2,1,0:T(8,128)(2,1)S(1)} %shard_map.46.made), custom_call_target="tpu_custom_call" | custom-call | tf_op jit(solution)/shard_map/pallas_call | solution.py:352

commit v3 on v2

--- a/solution.py
+++ b/solution.py
@@ -18,9 +18,9 @@
 
 def kernel(
     n_dom, n_grp, zagg, xlen, a_hbm, p_hbm, done,
-    a, p, pt, rt, ert, v, xv, below, above, left, right,
-    carry_out, carry_in, last,
-    a_sem, p_sem, z_send, z_recv, x_send, x_recv, c_send, c_recv,
+    a, p, pt, v, xv, below, above, left, right,
+    carry_out, carry_in, last, tile_out, tile_in, ev, late_out, late_in,
+    a_sem, p_sem, z_send, z_recv, x_send, x_recv, c_send, c_recv, k_send, k_recv, l_send, l_recv,
 ):
     layers, depth, columns, block, width = p.shape
     chunk = columns // 3
@@ -46,20 +46,10 @@
         half = pl.ds(h * (columns // 2), columns // 2)
         return pltpu.make_async_copy(p_hbm.at[z, :, half], p.at[z, :, half], p_sem.at[z, h])
 
-    order = [*range(1, layers - 1), 0, layers - 1]
+    order = [1, 0, *range(2, layers)]
     for z in range(3):
         p_copy(z, 0).start()
     a_copy(1, 0).start()
-    for z in range(3):
-        p_copy(z, 1).start()
-    a_copy(1, 1).start()
-    a_copy(1, 2).start()
-    for z in range(3, layers):
-        p_copy(z, 0).start()
-        p_copy(z, 1).start()
-    for z in order[1:]:
-        for t in range(3):
-            a_copy(z, t).start()
 
     barrier = pltpu.get_barrier_semaphore()
     for there, device in sides:
@@ -86,6 +76,8 @@
     rightward = remote(p_hbm.at[:, :, columns - 1], left, x_send.at[0], x_recv.at[0], (dom, grp + 1))
     leftward = remote(p_hbm.at[:, :, 0], right, x_send.at[1], x_recv.at[1], (dom, grp - 1))
     carry = remote(carry_out, carry_in, c_send, c_recv, (dom - 1, grp))
+    tiles = remote(tile_out, tile_in, k_send, k_recv, (dom + 1, grp))
+    late = remote(late_out, late_in, l_send, l_recv, (dom - 1, grp))
 
     @pl.when(has_above)
     def _():
@@ -94,7 +86,7 @@
 
     @pl.when(has_below)
     def _():
-        for t in range(3):
+        for t in range(2):
             down_third(t).start()
 
     @pl.when(has_right)
@@ -105,11 +97,15 @@
     def _():
         leftward.start()
 
-    for there, ref in ((has_below, below), (has_above, above), (has_left, left), (has_right, right), (has_above, carry_in)):
+    for there, ref in ((has_below, below), (has_above, above), (has_left, left), (has_right, right), (has_above, carry_in),
+                       (has_above, late_in), (has_below, tile_in)):
         @pl.when(jnp.logical_not(there))
         def _(ref=ref):
             for first in range(ref.shape[0]):
                 ref[first] = jnp.zeros(ref.shape[1:], ref.dtype)
+
+    for y in range(depth):
+        above[y, 2 * chunk :] = jnp.zeros((chunk, block, width), BF)
 
     one, none = jnp.int32(1), jnp.int32(0)
 
@@ -140,19 +136,17 @@
     rows = [slice(y * block, (y + 1) * block) for y in range(depth)]
 
     def main(z):
-        slots = 3 * width
+        slots = (3 if z > 0 else 2) * width
 
         def over(y, x):
             return p[z + 1, y, x] if z < layers - 1 else above[y, x]
-
-        def under(y, x):
-            return p[z - 1, y, x] if z > 0 else below[y, x]
 
         def first(x, slot):
             same_xm = (1.0 - real(column_begins(x))).astype(BF)
             same_xp = (1.0 - real(column_begins(x + 1))).astype(BF)
             xm, xp = jnp.maximum(x - 1, 0), jnp.minimum(x + 1, columns - 1)
             zero = jnp.zeros((block, width), BF)
+            out = []
             for y in range(depth):
                 stack = jnp.concatenate(
                     [
@@ -164,77 +158,130 @@
                     ],
                     axis=0,
                 )
-                rt[slot, rows[y], 0:width] = product(a[z, y, x, :, 0 : 5 * block], stack).astype(BF)
-                rt[slot, rows[y], width : 2 * width] = product(
-                    a[z, y, x, :, 6 * block : 7 * block], over(y, x)
-                ).astype(BF)
-                rt[slot, rows[y], 2 * width : slots] = product(
-                    a[z, y, x, :, 5 * block : 6 * block], under(y, x)
-                ).astype(BF)
-
-        def second(x, slot):
+                parts = [
+                    product(a[z, y, x, :, 0 : 5 * block], stack),
+                    product(a[z, y, x, :, 6 * block : 7 * block], over(y, x)),
+                ]
+                if z > 0:
+                    parts.append(product(a[z, y, x, :, 5 * block : 6 * block], p[z - 1, y, x]))
+                out.append(jnp.concatenate(parts, axis=1).astype(BF))
+            return jnp.concatenate(out, axis=0)
+
+        def second(x, routed):
             turned = jnp.concatenate([p[z, y, x] for y in range(depth)], axis=0).T
             pt[z, x] = turned
-            coarse = product(turned, rt[slot, :, 0:slots])
+            coarse = product(turned, routed)
             before = v[z, jnp.maximum(x - 1, 0), :, 0:slots]
             v[z, x, :, 0:slots] = coarse + jnp.where(column_begins(x) == 1, 0.0, before)
 
         def step(j, _):
-            if z in order[:-2]:
+            if z in order[:2]:
                 a_copy(z, j).wait()
             if z == order[0]:
+                @pl.when(j == 0)
+                def _():
+                    for other in range(3):
+                        p_copy(other, 1).start()
+                    a_copy(z, 1).start()
+                    a_copy(z, 2).start()
+
                 @pl.when(j == 1)
                 def _():
                     for other in range(3):
                         p_copy(other, 1).wait()
-            if z == 0:
-                @pl.when(has_below)
+                    for other in range(3, layers):
+                        p_copy(other, 0).start()
+                        p_copy(other, 1).start()
+                    for t in range(3):
+                        a_copy(order[1], t).start()
+
+                @pl.when(j == 2)
                 def _():
-                    up_third(j).wait_recv()
+                    for other in order[2:]:
+                        for t in range(3):
+                            a_copy(other, t).start()
             if z == layers - 1:
-                @pl.when(has_above)
+                @pl.when(jnp.logical_and(has_above, j < 2))
                 def _():
                     down_third(j).wait_recv()
+            held = None
             for u in range(UNROLL):
-                first(j * UNROLL + u, u)
+                made = first(j * UNROLL + u, u)
                 if u > 0:
-                    second(j * UNROLL + u - 1, u - 1)
-            second(j * UNROLL + UNROLL - 1, UNROLL - 1)
+                    second(j * UNROLL + u - 1, held)
+                held = made
+            second(j * UNROLL + UNROLL - 1, held)
             return 0
 
         lax.fori_loop(0, columns // UNROLL, step, 0)
 
-    def x_sides(z, at):
+    def x_sides(z):
         for i in range(1, intervals):
             hi = jnp.clip(cuts[i], 1, columns - 1)
             lo = hi - 1
-            for y in range(depth):
-                ert[at, rows[y]] = product(a[z, y, lo, :, 2 * block : 3 * block], p[z, y, hi]).astype(BF)
-                ert[at + 1, rows[y]] = product(a[z, y, hi, :, block : 2 * block], p[z, y, lo]).astype(BF)
-            xv[1, z, i - 1] = product(pt[z, lo], ert[at])
-            xv[0, z, i] = product(pt[z, hi], ert[at + 1])
-            at += 2
-        for y in range(depth):
-            ert[at, rows[y]] = product(a[z, y, columns - 1, :, 2 * block : 3 * block], right[z, y]).astype(BF)
-            ert[at + 1, rows[y]] = product(a[z, y, 0, :, block : 2 * block], left[z, y]).astype(BF)
-        xv[1, z, intervals - 1] = product(pt[z, columns - 1], ert[at])
-        xv[0, z, 0] = product(pt[z, 0], ert[at + 1])
+            low = jnp.concatenate(
+                [product(a[z, y, lo, :, 2 * block : 3 * block], p[z, y, hi]).astype(BF) for y in range(depth)], axis=0
+            )
+            high = jnp.concatenate(
+                [product(a[z, y, hi, :, block : 2 * block], p[z, y, lo]).astype(BF) for y in range(depth)], axis=0
+            )
+            xv[1, z, i - 1] = product(pt[z, lo], low)
+            xv[0, z, i] = product(pt[z, hi], high)
+        low = jnp.concatenate(
+            [product(a[z, y, columns - 1, :, 2 * block : 3 * block], right[z, y]).astype(BF) for y in range(depth)], axis=0
+        )
+        high = jnp.concatenate(
+            [product(a[z, y, 0, :, block : 2 * block], left[z, y]).astype(BF) for y in range(depth)], axis=0
+        )
+        xv[1, z, intervals - 1] = product(pt[z, columns - 1], low)
+        xv[0, z, 0] = product(pt[z, 0], high)
+
+    def edge(t):
+        @pl.when(has_below)
+        def _():
+            up_third(t).wait_recv()
+        for x in range(t * chunk, (t + 1) * chunk):
+            beside = jnp.concatenate(
+                [product(a[0, y, x, :, 5 * block : 6 * block], below[y, x]).astype(BF) for y in range(depth)], axis=0
+            )
+            coarse = product(pt[0, x], beside)
+            if x > 0:
+                coarse = coarse + jnp.where(column_begins(x) == 1, 0.0, v[0, x - 1, :, 2 * width :])
+            v[0, x, :, 2 * width :] = coarse
+
+    def edge_of_below():
+        @pl.when(has_below)
+        def _():
+            tiles.wait_recv()
+        for u in range(chunk):
+            x, half = 2 * chunk + u, u % 2 * block
+            beside = jnp.concatenate(
+                [product(tile_in[y, u // 2, :, half : half + block], p[0, y, x]).astype(BF) for y in range(depth)],
+                axis=0,
+            )
+            turned = jnp.concatenate([below[y, x] for y in range(depth)], axis=0).T
+            coarse = product(turned, beside)
+            if u > 0:
+                coarse = coarse + jnp.where(column_begins(x) == 1, 0.0, ev[u - 1])
+            ev[u] = coarse
 
     S = [slice(k * width, (k + 1) * width) for k in range(5)]
 
-    def layer_slots(z, i):
+    def layer_slots(z, i, early=False):
         end = jnp.clip(cuts[i + 1] - 1, 0, columns - 1)
         own = v[z, end, :, S[0]]
         zp, zm = v[z, end, :, S[1]], v[z, end, :, S[2]]
         here, there = real(begins[z]), real(begins[z + 1])
+        if early and z == 0:
+            return own + (1.0 - there) * zp, xv[0, z, i], xv[1, z, i], None, there * zp
         own = own + (1.0 - here) * zm + (1.0 - there) * zp
         return own, xv[0, z, i], xv[1, z, i], here * zm, there * zp
 
-    def gathered(i, zs, wanted, slots):
+    def gathered(i, zs, wanted, slots, early=False):
         total = None
         for z in zs:
             w = real(jnp.where(group[z] == wanted, one, none))
-            terms = layer_slots(z, i)
+            terms = layer_slots(z, i, early)
             terms = [terms[s] * w for s in slots]
             total = terms if total is None else [t + u for t, u in zip(total, terms)]
         return total
@@ -242,63 +289,94 @@
     for z in range(3):
         p_copy(z, 0).wait()
     main(1)
+    main(0)
     for z in range(3, layers):
         p_copy(z, 0).wait()
         p_copy(z, 1).wait()
-    for z in order[1:-2]:
+
+    for z in order[2:]:
+        for t in range(3):
+            a_copy(z, t).wait()
+    for y in range(depth):
+        for q in range(chunk // 2):
+            x = 2 * chunk + 2 * q
+            tile_out[y, q] = jnp.concatenate(
+                [a[layers - 1, y, x + n, :, 6 * block : 7 * block] for n in range(2)], axis=1
+            )
+
+    @pl.when(has_above)
+    def _():
+        tiles.start()
+
+    @pl.when(has_left)
+    def _():
+        rightward.wait_recv()
+
+    @pl.when(has_right)
+    def _():
+        leftward.wait_recv()
+
+    x_sides(0)
+    x_sides(1)
+    for i in range(intervals):
+        for s, term in enumerate(gathered(i, (0, 1), 0, (0, 1, 2, 4), True)):
+            carry_out[i, :, S[s]] = term.astype(BF)
+
+    @pl.when(has_below)
+    def _():
+        carry.start()
+
+    for z in order[2:-1]:
         main(z)
-
-    @pl.when(has_left)
-    def _():
-        rightward.wait_recv()
-
-    @pl.when(has_right)
-    def _():
-        leftward.wait_recv()
-
-    for t in range(3):
-        a_copy(0, t).wait()
-        a_copy(layers - 1, t).wait()
-    for n, z in enumerate(order[:-2]):
-        x_sides(z, 2 * intervals * n)
-    main(0)
-    x_sides(0, 0)
-    for i in range(intervals):
-        for s, term in enumerate(gathered(i, (0, 1), 0, (0, 1, 2, 4))):
-            carry_out[i, :, S[s]] = term.astype(BF)
+        x_sides(z)
+    edge(0)
+    edge(1)
+    main(layers - 1)
+    x_sides(layers - 1)
+    for i in range(intervals):
+        for s, term in enumerate(gathered(i, range(1, layers), 2, range(5))):
+            last[i, :, S[s]] = term
+    edge(2)
+    edge_of_below()
+    for i in range(intervals):
+        end = jnp.clip(cuts[i + 1] - 1, 0, columns - 1)
+        mine = (1.0 - real(begins[0])) * v[0, end, :, S[2]]
+        theirs = ev[jnp.maximum(end - 2 * chunk, 0)]
+        late_out[i] = (mine + real(jnp.where(end >= 2 * chunk, one, none)) * theirs).astype(BF)
 
     @pl.when(has_below)
     def _():
-        carry.start()
-
-    main(layers - 1)
-    x_sides(layers - 1, 0)
+        late.start()
+
     for i in range(intervals):
         for s, term in enumerate(gathered(i, range(layers - 1), 1, range(5))):
             done[0, i, :, S[s]] = term.astype(BF)
-    for i in range(intervals):
-        for s, term in enumerate(gathered(i, range(1, layers), 2, range(5))):
-            last[i, :, S[s]] = term
 
     @pl.when(has_above)
     def _():
         carry.wait_recv()
-
-    for i in range(intervals):
-        for s, c in ((0, 0), (1, 1), (2, 2), (4, 3)):
-            done[1, i, :, S[s]] = (last[i, :, S[s]] + carry_in[i, :, S[c]].astype(F32)).astype(BF)
+        late.wait_recv()
+
+    parted = real(begins[layers])
+    for i in range(intervals):
+        more = late_in[i].astype(F32)
+        for s, c, w in ((0, 0, 1.0 - parted), (1, 1, None), (2, 2, None), (4, 3, parted)):
+            term = last[i, :, S[s]] + carry_in[i, :, S[c]].astype(F32)
+            done[1, i, :, S[s]] = (term if w is None else term + w * more).astype(BF)
         done[1, i, :, S[3]] = last[i, :, S[3]].astype(BF)
 
     @pl.when(has_above)
     def _():
         for t in range(3):
             up_third(t).wait_send()
+        tiles.wait_send()
 
     @pl.when(has_below)
     def _():
-        for t in range(3):
+        for t in range(2):
             down_third(t).wait_send()
         carry.wait_send()
+        late.wait_send()
 
     @pl.when(has_right)
     def _():
@@ -331,8 +409,6 @@
             vm(a_blocks.shape, BF),
             vm(prolong.shape, BF),
             vm((layers, columns, width, long), BF),
-            vm((UNROLL, long, 3 * width), BF),
-            vm((4 * intervals, long, width), BF),
             vm((layers, columns, width, 3 * width), F32),
             vm((2, layers, intervals, width, width), F32),
             vm(prolong.shape[1:], BF),
@@ -342,8 +418,13 @@
             vm((intervals, width, 4 * width), BF),
             vm((intervals, width, 4 * width), BF),
             vm((intervals, width, 5 * width), F32),
+            vm((depth, columns // 6, block, 2 * block), BF),
+            vm((depth, columns // 6, block, 2 * block), BF),
+            vm((columns // 3, width, width), F32),
+            vm((intervals, width, width), BF),
+            vm((intervals, width, width), BF),
             dma((layers, 3)), dma((layers, 2)), dma((2, 3)), dma((2, 3)),
-            dma((2,)), dma((2,)), dma, dma,
+            dma((2,)), dma((2,)), dma, dma, dma, dma, dma, dma,
         ],
         compiler_params=pltpu.CompilerParams(
             collective_id=0, has_side_effects=True, vmem_limit_bytes=60 * 2**20

time: 33.9 us -> 38.1 us (1.12)
  the two profiles are of different devices: /device:TPU:27 before, /device:TPU:1 now
where the time goes in v3:
time: 38.1 us; the launch traced here: 38 us
  Pallas kernels  37.9 us (99%)
    pallas_call x1, Pallas kernels, per_device(): pl.pallas_call(functools.partial(kernel, n_dom, n_grp), out_shape=vm((lay...  36.8 us
    pallas_call x1, Pallas kernels, per_device(): pl.pallas_call(settle, out_shape=jax.ShapeDtypeStruct(made.shape, BF), in...  1.12 us

profile of v3, /device:TPU:1, one launch (start us, length us, event | category | flops | bytes accessed | tf_op | source)
XLA Modules:
  0.0 38.0 jit_solution(3187466998224572870)
XLA Ops:
  0.0 36.8 %shard_map.46.made = bf16[2,4,128,640]{3,2,1,0:T(8,128)(2,1)S(1)} custom-call(s32[128]{0:T(128)} %zagg.1, s32[4,4]{1,0:T(4,128)} %xlen.1, bf16[4,7,12,64,448]{4,3,2,1,0:T(8,128)(2,1)} %a_hbm.1, bf16[4,7,12,64,128]{4,3,2,1,0:T(8,128)(2,1)} %p_hbm.1), custom_call_target="tpu_custom_call" | custom-call | tf_op jit(solution)/shard_map/pallas_call | solution.py:403
  36.8 1.1 %shard_map.47 = bf16[2,4,128,640]{3,2,1,0:T(8,128)(2,1)} custom-call(bf16[2,4,128,640]{3,2,1,0:T(8,128)(2,1)S(1)} %shard_map.46.made), custom_call_target="tpu_custom_call" | custom-call | tf_op jit(solution)/shard_map/pallas_call | solution.py:433

commit v4 on v3

--- a/solution.py
+++ b/solution.py
@@ -19,8 +19,8 @@
 def kernel(
     n_dom, n_grp, zagg, xlen, a_hbm, p_hbm, done,
     a, p, pt, v, xv, below, above, left, right,
-    carry_out, carry_in, last, tile_out, tile_in, ev, late_out, late_in,
-    a_sem, p_sem, z_send, z_recv, x_send, x_recv, c_send, c_recv, k_send, k_recv, l_send, l_recv,
+    carry_out, carry_in, last, late_out, late_in,
+    a_sem, p_sem, z_send, z_recv, x_send, x_recv, c_send, c_recv, l_send, l_recv,
 ):
     layers, depth, columns, block, width = p.shape
     chunk = columns // 3
@@ -46,7 +46,7 @@
         half = pl.ds(h * (columns // 2), columns // 2)
         return pltpu.make_async_copy(p_hbm.at[z, :, half], p.at[z, :, half], p_sem.at[z, h])
 
-    order = [1, 0, *range(2, layers)]
+    order = [*range(1, layers - 1), 0, layers - 1]
     for z in range(3):
         p_copy(z, 0).start()
     a_copy(1, 0).start()
@@ -76,7 +76,6 @@
     rightward = remote(p_hbm.at[:, :, columns - 1], left, x_send.at[0], x_recv.at[0], (dom, grp + 1))
     leftward = remote(p_hbm.at[:, :, 0], right, x_send.at[1], x_recv.at[1], (dom, grp - 1))
     carry = remote(carry_out, carry_in, c_send, c_recv, (dom - 1, grp))
-    tiles = remote(tile_out, tile_in, k_send, k_recv, (dom + 1, grp))
     late = remote(late_out, late_in, l_send, l_recv, (dom - 1, grp))
 
     @pl.when(has_above)
@@ -86,7 +85,7 @@
 
     @pl.when(has_below)
     def _():
-        for t in range(2):
+        for t in range(3):
             down_third(t).start()
 
     @pl.when(has_right)
@@ -98,14 +97,11 @@
         leftward.start()
 
     for there, ref in ((has_below, below), (has_above, above), (has_left, left), (has_right, right), (has_above, carry_in),
-                       (has_above, late_in), (has_below, tile_in)):
+                       (has_above, late_in)):
         @pl.when(jnp.logical_not(there))
         def _(ref=ref):
             for first in range(ref.shape[0]):
                 ref[first] = jnp.zeros(ref.shape[1:], ref.dtype)
-
-    for y in range(depth):
-        above[y, 2 * chunk :] = jnp.zeros((chunk, block, width), BF)
 
     one, none = jnp.int32(1), jnp.int32(0)
 
@@ -135,11 +131,14 @@
 
     rows = [slice(y * block, (y + 1) * block) for y in range(depth)]
 
-    def main(z):
-        slots = (3 if z > 0 else 2) * width
+    def main(z, begin=0, end=3, low=True):
+        slots = (3 if low else 2) * width
 
         def over(y, x):
             return p[z + 1, y, x] if z < layers - 1 else above[y, x]
+
+        def under(y, x):
+            return p[z - 1, y, x] if z > 0 else below[y, x]
 
         def first(x, slot):
             same_xm = (1.0 - real(column_begins(x))).astype(BF)
@@ -162,8 +161,8 @@
                     product(a[z, y, x, :, 0 : 5 * block], stack),
                     product(a[z, y, x, :, 6 * block : 7 * block], over(y, x)),
                 ]
-                if z > 0:
-                    parts.append(product(a[z, y, x, :, 5 * block : 6 * block], p[z - 1, y, x]))
+                if low:
+                    parts.append(product(a[z, y, x, :, 5 * block : 6 * block], under(y, x)))
                 out.append(jnp.concatenate(parts, axis=1).astype(BF))
             return jnp.concatenate(out, axis=0)
 
@@ -175,7 +174,7 @@
             v[z, x, :, 0:slots] = coarse + jnp.where(column_begins(x) == 1, 0.0, before)
 
         def step(j, _):
-            if z in order[:2]:
+            if z in order[:-2]:
                 a_copy(z, j).wait()
             if z == order[0]:
                 @pl.when(j == 0)
@@ -200,8 +199,12 @@
                     for other in order[2:]:
                         for t in range(3):
                             a_copy(other, t).start()
+            if z == 0 and low:
+                @pl.when(has_below)
+                def _():
+                    up_third(j).wait_recv()
             if z == layers - 1:
-                @pl.when(jnp.logical_and(has_above, j < 2))
+                @pl.when(has_above)
                 def _():
                     down_third(j).wait_recv()
             held = None
@@ -213,7 +216,7 @@
             second(j * UNROLL + UNROLL - 1, held)
             return 0
 
-        lax.fori_loop(0, columns // UNROLL, step, 0)
+        lax.fori_loop(begin, end, step, 0)
 
     def x_sides(z):
         for i in range(1, intervals):
@@ -227,6 +230,7 @@
             )
             xv[1, z, i - 1] = product(pt[z, lo], low)
             xv[0, z, i] = product(pt[z, hi], high)
+    def outer_sides(z):
         low = jnp.concatenate(
             [product(a[z, y, columns - 1, :, 2 * block : 3 * block], right[z, y]).astype(BF) for y in range(depth)], axis=0
         )
@@ -249,22 +253,6 @@
                 coarse = coarse + jnp.where(column_begins(x) == 1, 0.0, v[0, x - 1, :, 2 * width :])
             v[0, x, :, 2 * width :] = coarse
 
-    def edge_of_below():
-        @pl.when(has_below)
-        def _():
-            tiles.wait_recv()
-        for u in range(chunk):
-            x, half = 2 * chunk + u, u % 2 * block
-            beside = jnp.concatenate(
-                [product(tile_in[y, u // 2, :, half : half + block], p[0, y, x]).astype(BF) for y in range(depth)],
-                axis=0,
-            )
-            turned = jnp.concatenate([below[y, x] for y in range(depth)], axis=0).T
-            coarse = product(turned, beside)
-            if u > 0:
-                coarse = coarse + jnp.where(column_begins(x) == 1, 0.0, ev[u - 1])
-            ev[u] = coarse
-
     S = [slice(k * width, (k + 1) * width) for k in range(5)]
 
     def layer_slots(z, i, early=False):
@@ -289,25 +277,20 @@
     for z in range(3):
         p_copy(z, 0).wait()
     main(1)
-    main(0)
     for z in range(3, layers):
         p_copy(z, 0).wait()
         p_copy(z, 1).wait()
-
-    for z in order[2:]:
-        for t in range(3):
-            a_copy(z, t).wait()
-    for y in range(depth):
-        for q in range(chunk // 2):
-            x = 2 * chunk + 2 * q
-            tile_out[y, q] = jnp.concatenate(
-                [a[layers - 1, y, x + n, :, 6 * block : 7 * block] for n in range(2)], axis=1
-            )
-
-    @pl.when(has_above)
-    def _():
-        tiles.start()
-
+    for z in order[1:-2]:
+        main(z)
+
+    for t in range(3):
+        a_copy(0, t).wait()
+        a_copy(layers - 1, t).wait()
+    for z in order[:-2]:
+        x_sides(z)
+    main(0, 0, 2)
+    main(0, 2, 3, False)
+    x_sides(0)
     @pl.when(has_left)
     def _():
         rightward.wait_recv()
@@ -316,8 +299,8 @@
     def _():
         leftward.wait_recv()
 
-    x_sides(0)
-    x_sides(1)
+    outer_sides(0)
+    outer_sides(1)
     for i in range(intervals):
         for s, term in enumerate(gathered(i, (0, 1), 0, (0, 1, 2, 4), True)):
             carry_out[i, :, S[s]] = term.astype(BF)
@@ -326,54 +309,47 @@
     def _():
         carry.start()
 
-    for z in order[2:-1]:
-        main(z)
-        x_sides(z)
-    edge(0)
-    edge(1)
-    main(layers - 1)
+    main(layers - 1, 0, 2)
+    for z in order[1:-2]:
+        outer_sides(z)
+    edge(2)
+    for i in range(intervals):
+        end = jnp.clip(cuts[i + 1] - 1, 0, columns - 1)
+        late_out[i] = ((1.0 - real(begins[0])) * v[0, end, :, S[2]]).astype(BF)
+
+    @pl.when(has_below)
+    def _():
+        late.start()
+
+    main(layers - 1, 2, 3)
     x_sides(layers - 1)
+    outer_sides(layers - 1)
+    for i in range(intervals):
+        for s, term in enumerate(gathered(i, range(layers - 1), 1, range(5))):
+            done[0, i, :, S[s]] = term.astype(BF)
     for i in range(intervals):
         for s, term in enumerate(gathered(i, range(1, layers), 2, range(5))):
             last[i, :, S[s]] = term
-    edge(2)
-    edge_of_below()
-    for i in range(intervals):
-        end = jnp.clip(cuts[i + 1] - 1, 0, columns - 1)
-        mine = (1.0 - real(begins[0])) * v[0, end, :, S[2]]
-        theirs = ev[jnp.maximum(end - 2 * chunk, 0)]
-        late_out[i] = (mine + real(jnp.where(end >= 2 * chunk, one, none)) * theirs).astype(BF)
-
-    @pl.when(has_below)
-    def _():
-        late.start()
-
-    for i in range(intervals):
-        for s, term in enumerate(gathered(i, range(layers - 1), 1, range(5))):
-            done[0, i, :, S[s]] = term.astype(BF)
 
     @pl.when(has_above)
     def _():
         carry.wait_recv()
         late.wait_recv()
 
-    parted = real(begins[layers])
-    for i in range(intervals):
-        more = late_in[i].astype(F32)
-        for s, c, w in ((0, 0, 1.0 - parted), (1, 1, None), (2, 2, None), (4, 3, parted)):
+    for i in range(intervals):
+        for s, c in ((0, 0), (1, 1), (2, 2), (4, 3)):
             term = last[i, :, S[s]] + carry_in[i, :, S[c]].astype(F32)
-            done[1, i, :, S[s]] = (term if w is None else term + w * more).astype(BF)
+            done[1, i, :, S[s]] = (term + late_in[i].astype(F32) if s == 0 else term).astype(BF)
         done[1, i, :, S[3]] = last[i, :, S[3]].astype(BF)
 
     @pl.when(has_above)
     def _():
         for t in range(3):
             up_third(t).wait_send()
-        tiles.wait_send()
 
     @pl.when(has_below)
     def _():
-        for t in range(2):
+        for t in range(3):
             down_third(t).wait_send()
         carry.wait_send()
         late.wait_send()
@@ -418,13 +394,10 @@
             vm((intervals, width, 4 * width), BF),
             vm((intervals, width, 4 * width), BF),
             vm((intervals, width, 5 * width), F32),
-            vm((depth, columns // 6, block, 2 * block), BF),
-            vm((depth, columns // 6, block, 2 * block), BF),
-            vm((columns // 3, width, width), F32),
             vm((intervals, width, width), BF),
             vm((intervals, width, width), BF),
             dma((layers, 3)), dma((layers, 2)), dma((2, 3)), dma((2, 3)),
-            dma((2,)), dma((2,)), dma, dma, dma, dma, dma, dma,
+            dma((2,)), dma((2,)), dma, dma, dma, dma,
         ],
         compiler_params=pltpu.CompilerParams(
             collective_id=0, has_side_effects=True, vmem_limit_bytes=60 * 2**20

time: 38.1 us -> 31.4 us (0.82)
  the two profiles are of different devices: /device:TPU:1 before, /device:TPU:27 now
where the time goes in v4:
time: 31.4 us; the launch traced here: 31.3 us
  Pallas kernels  31.3 us (100%)
    pallas_call x1, Pallas kernels, per_device(): pl.pallas_call(functools.partial(kernel, n_dom, n_grp), out_shape=vm((lay...  30.2 us
    pallas_call x1, Pallas kernels, per_device(): pl.pallas_call(settle, out_shape=jax.ShapeDtypeStruct(made.shape, BF), in...  1.12 us

profile of v4, /device:TPU:27, one launch (start us, length us, event | category | flops | bytes accessed | tf_op | source)
XLA Modules:
  0.0 31.3 jit_solution(13296547835621647683)
XLA Ops:
  0.0 30.2 %shard_map.46.made = bf16[2,4,128,640]{3,2,1,0:T(8,128)(2,1)S(1)} custom-call(s32[128]{0:T(128)} %zagg.1, s32[4,4]{1,0:T(4,128)} %xlen.1, bf16[4,7,12,64,448]{4,3,2,1,0:T(8,128)(2,1)} %a_hbm.1, bf16[4,7,12,64,128]{4,3,2,1,0:T(8,128)(2,1)} %p_hbm.1), custom_call_target="tpu_custom_call" | custom-call | tf_op jit(solution)/shard_map/pallas_call | solution.py:379
  30.2 1.1 %shard_map.47 = bf16[2,4,128,640]{3,2,1,0:T(8,128)(2,1)} custom-call(bf16[2,4,128,640]{3,2,1,0:T(8,128)(2,1)S(1)} %shard_map.46.made), custom_call_target="tpu_custom_call" | custom-call | tf_op jit(solution)/shard_map/pallas_call | solution.py:406

commit v5 on v4

--- a/solution.py
+++ b/solution.py
@@ -286,11 +286,23 @@
     for t in range(3):
         a_copy(0, t).wait()
         a_copy(layers - 1, t).wait()
-    for z in order[:-2]:
-        x_sides(z)
+    x_sides(1)
     main(0, 0, 2)
     main(0, 2, 3, False)
     x_sides(0)
+    sent = [(s, i) for s in range(4) for i in range(intervals) if (s, i) not in ((1, 0), (2, intervals - 1))]
+    tile_of = {key: n for n, key in enumerate(sent)}
+    for i in range(intervals):
+        for s, term in enumerate(gathered(i, (0, 1), 0, (0, 1, 2, 4), True)):
+            if (s, i) in tile_of:
+                carry_out[tile_of[s, i]] = term.astype(BF)
+
+    @pl.when(has_below)
+    def _():
+        carry.start()
+
+    for z in order[1:-2]:
+        x_sides(z)
     @pl.when(has_left)
     def _():
         rightward.wait_recv()
@@ -299,29 +311,23 @@
     def _():
         leftward.wait_recv()
 
-    outer_sides(0)
-    outer_sides(1)
-    for i in range(intervals):
-        for s, term in enumerate(gathered(i, (0, 1), 0, (0, 1, 2, 4), True)):
-            carry_out[i, :, S[s]] = term.astype(BF)
-
-    @pl.when(has_below)
-    def _():
-        carry.start()
-
-    main(layers - 1, 0, 2)
-    for z in order[1:-2]:
+    for z in range(layers - 1):
         outer_sides(z)
     edge(2)
     for i in range(intervals):
         end = jnp.clip(cuts[i + 1] - 1, 0, columns - 1)
         late_out[i] = ((1.0 - real(begins[0])) * v[0, end, :, S[2]]).astype(BF)
 
+    for side, at in ((0, 0), (1, intervals - 1)):
+        late_out[intervals + side] = sum(
+            real(jnp.where(group[z] == 0, one, none)) * xv[side, z, at] for z in range(2)
+        ).astype(BF)
+
     @pl.when(has_below)
     def _():
         late.start()
 
-    main(layers - 1, 2, 3)
+    main(layers - 1)
     x_sides(layers - 1)
     outer_sides(layers - 1)
     for i in range(intervals):
@@ -338,8 +344,16 @@
 
     for i in range(intervals):
         for s, c in ((0, 0), (1, 1), (2, 2), (4, 3)):
-            term = last[i, :, S[s]] + carry_in[i, :, S[c]].astype(F32)
-            done[1, i, :, S[s]] = (term + late_in[i].astype(F32) if s == 0 else term).astype(BF)
+            term = last[i, :, S[s]]
+            if (c, i) in tile_of:
+                term = term + carry_in[tile_of[c, i]].astype(F32)
+            if s == 0:
+                term = term + late_in[i].astype(F32)
+            if s == 1 and i == 0:
+                term = term + late_in[intervals].astype(F32)
+            if s == 2 and i == intervals - 1:
+                term = term + late_in[intervals + 1].astype(F32)
+            done[1, i, :, S[s]] = term.astype(BF)
         done[1, i, :, S[3]] = last[i, :, S[3]].astype(BF)
 
     @pl.when(has_above)
@@ -391,11 +405,11 @@
             vm(prolong.shape[1:], BF),
             vm((layers, depth, block, width), BF),
             vm((layers, depth, block, width), BF),
-            vm((intervals, width, 4 * width), BF),
-            vm((intervals, width, 4 * width), BF),
+            vm((4 * intervals - 2, width, width), BF),
+            vm((4 * intervals - 2, width, width), BF),
             vm((intervals, width, 5 * width), F32),
-            vm((intervals, width, width), BF),
-            vm((intervals, width, width), BF),
+            vm((intervals + 2, width, width), BF),
+            vm((intervals + 2, width, width), BF),
             dma((layers, 3)), dma((layers, 2)), dma((2, 3)), dma((2, 3)),
             dma((2,)), dma((2,)), dma, dma, dma, dma,
         ],

time: 31.4 us -> 30.7 us (0.978)
  Pallas kernels: 31.3 us -> 30.5 us
    pallas_call x1, Pallas kernels: 30.2 us -> 29.4 us  [per_device(): pl.pallas_call(functools.partial(kernel, n_dom, n_grp), out_shape=vm((lay...]
where the time goes in v5:
time: 30.7 us; the launch traced here: 30.6 us
  Pallas kernels  30.5 us (99%)
    pallas_call x1, Pallas kernels, per_device(): pl.pallas_call(functools.partial(kernel, n_dom, n_grp), out_shape=vm((lay...  29.4 us
    pallas_call x1, Pallas kernels, per_device(): pl.pallas_call(settle, out_shape=jax.ShapeDtypeStruct(made.shape, BF), in...  1.12 us

profile of v5, /device:TPU:27, one launch (start us, length us, event | category | flops | bytes accessed | tf_op | source)
XLA Modules:
  0.0 30.6 jit_solution(11508625816395643589)
XLA Ops:
  0.0 29.4 %shard_map.46.made = bf16[2,4,128,640]{3,2,1,0:T(8,128)(2,1)S(1)} custom-call(s32[128]{0:T(128)} %zagg.1, s32[4,4]{1,0:T(4,128)} %xlen.1, bf16[4,7,12,64,448]{4,3,2,1,0:T(8,128)(2,1)} %a_hbm.1, bf16[4,7,12,64,128]{4,3,2,1,0:T(8,128)(2,1)} %p_hbm.1), custom_call_target="tpu_custom_call" | custom-call | tf_op jit(solution)/shard_map/pallas_call | solution.py:393
  29.4 1.1 %shard_map.47 = bf16[2,4,128,640]{3,2,1,0:T(8,128)(2,1)} custom-call(bf16[2,4,128,640]{3,2,1,0:T(8,128)(2,1)S(1)} %shard_map.46.made), custom_call_target="tpu_custom_call" | custom-call | tf_op jit(solution)/shard_map/pallas_call | solution.py:420
